TPU v7x, 32 devices: a whole 2x2x4 slice. The times are simulated.
32 devices in a mesh: dp: 8 (over y, x, core), mp: 4 (over z).
Axes of the slice: x: 2, y: 2, z: 4, core: 2. Of those that a mesh axis runs over, the one named last changes fastest.
Arguments:
- inputs: bfloat16 [10240, 768], P(('dp', 'mp')), may hold values from -6 to 6
- lengths: int32 [16], P('dp'), may hold values from 50 to 577, as said below
- cotangent: bfloat16 [10240, 768], P(('dp', 'mp')), may hold values from -12 to 12
- student_gains: float32 [2, 768], replicated, may hold values from 0.1 to 1.9
- student_shifts: float32 [2, 768], replicated, may hold values from -3 to 3
- student_project_in: bfloat16 [3, 768, 768], P(None, None, 'mp'), may hold values from -0.21875 to 0.21875
- student_project_bias: float32 [2, 768], P(None, 'mp'), may hold values from -3 to 3
- student_project_out: bfloat16 [768, 768], P('mp'), may hold values from -0.875 to 0.875
- student_out_bias: float32 [2, 768], replicated, may hold values from -3 to 3
- student_scales: float32 [2, 768], replicated, may hold values from 0.1 to 1.9
- student_up_weight: bfloat16 [768, 3072], P(None, 'mp'), may hold values from -0.21875 to 0.21875
- student_up_bias: float32 [3072], P('mp'), may hold values from -3 to 3
- student_down_weight: bfloat16 [3072, 768], P('mp'), may hold values from -0.109375 to 0.109375
- teacher_gains: float32 [2, 768], replicated, may hold values from 0.1 to 1.9
- teacher_shifts: float32 [2, 768], replicated, may hold values from -3 to 3
- teacher_project_in: bfloat16 [3, 768, 768], P(None, None, 'mp'), may hold values from -0.21875 to 0.21875
- teacher_project_bias: float32 [2, 768], P(None, 'mp'), may hold values from -3 to 3
- teacher_project_out: bfloat16 [768, 768], P('mp'), may hold values from -0.875 to 0.875
- teacher_out_bias: float32 [2, 768], replicated, may hold values from -3 to 3
- teacher_scales: float32 [2, 768], replicated, may hold values from 0.1 to 1.9
- teacher_up_weight: bfloat16 [768, 3072], P(None, 'mp'), may hold values from -0.21875 to 0.21875
- teacher_up_bias: float32 [3072], P('mp'), may hold values from -3 to 3
- teacher_down_weight: bfloat16 [3072, 768], P('mp'), may hold values from -0.109375 to 0.109375
Outputs:
- output: bfloat16 [10240, 768], P(('dp', 'mp'))
- input_grad: bfloat16 [10240, 768], P(('dp', 'mp'))
- student_gains_grad: float32 [2, 768], replicated
- student_shifts_grad: float32 [2, 768], replicated
- student_project_in_grad: float32 [3, 768, 768], P(None, None, 'mp')
- student_project_bias_grad: float32 [2, 768], P(None, 'mp')
- student_project_out_grad: float32 [768, 768], P('mp')
- student_out_bias_grad: float32 [2, 768], replicated
- student_scales_grad: float32 [2, 768], replicated
- student_up_weight_grad: float32 [768, 3072], P(None, 'mp')
- student_up_bias_grad: float32 [3072], P('mp')
- student_down_weight_grad: float32 [3072, 768], P('mp')
- teacher_gains_grad: float32 [2, 768], replicated
- teacher_shifts_grad: float32 [2, 768], replicated
- teacher_project_in_grad: float32 [3, 768, 768], P(None, None, 'mp')
- teacher_project_bias_grad: float32 [2, 768], P(None, 'mp')
- teacher_project_out_grad: float32 [768, 768], P('mp')
- teacher_out_bias_grad: float32 [2, 768], replicated
- teacher_scales_grad: float32 [2, 768], replicated
- teacher_up_weight_grad: float32 [768, 3072], P(None, 'mp')
- teacher_up_bias_grad: float32 [3072], P('mp')
- teacher_down_weight_grad: float32 [3072, 768], P('mp')
Inputs may be any that keep to these rules, and one draw needn't show every extreme that they name: `lengths`: in each aligned run of 2 images one image has exactly 577 rows.
All inputs are finite; a program needn't handle non-finite values.
Results may differ from a plain program's by a relative error of at most 0.03.
Values may be sent and summed in bfloat16 or wider, within the bound.
A program may use at most 128 MiB of HBM per device.

v0:
```python
import jax
import jax.numpy as jnp
from jax import lax
from jax.sharding import PartitionSpec as P

HEAD_DIM = 64
SLOT = 640


epsilon = 1e-06


def layer_norm(values, norm_gain, norm_shift):
    center = values - jnp.mean(values, axis=-1, keepdims=True)
    spread = jnp.mean(center * center, axis=-1, keepdims=True)
    return center * lax.rsqrt(spread + epsilon) * norm_gain + norm_shift


def gelu_exact(values):
    return jax.nn.gelu(values, approximate=False)


def matmul(left_side, right_side):
    return jnp.dot(left_side, right_side, preferred_element_type=jnp.float32)


def matmul_tn(left_side, right_side):
    return lax.dot_general(
        left_side, right_side, (((0,), (0,)), ((), ())), preferred_element_type=jnp.float32
    )


def matmul_nt(left_side, right_side):
    return lax.dot_general(
        left_side, right_side, (((1,), (1,)), ((), ())), preferred_element_type=jnp.float32
    )


def column_sums(values):
    return jnp.sum(values, axis=0, dtype=jnp.float32)


def gather_rows(source):
    return lax.all_gather(source, "mp", axis=0, tiled=True)


def gather_grads(source):
    return lax.all_gather(source, "mp", axis=0, tiled=True)


def branch_rows(source, weight):
    return lax.psum_scatter(
        matmul(source, weight).astype(jnp.bfloat16), "mp", scatter_dimension=0, tiled=True
    ).astype(jnp.float32)


def input_rows(grad_parts, weight_parts, local_rows):
    summed = jnp.zeros((local_rows * lax.axis_size("mp"), weight_parts[0].shape[0]), jnp.float32)
    for grad_part, weight in zip(grad_parts, weight_parts):
        summed = summed + matmul_nt(grad_part, weight)
    return lax.psum_scatter(
        summed.astype(jnp.bfloat16), "mp", scatter_dimension=0, tiled=True
    ).astype(jnp.float32)


def split_heads(values, image_count, head_count):
    return values.reshape(image_count, -1, head_count, HEAD_DIM)


def masked_scores(query_img, key_img, mask_row):
    scores = jnp.einsum(
        "qhd,khd->hqk", query_img, key_img, preferred_element_type=jnp.float32
    ) * HEAD_DIM ** (-0.5)
    return jnp.where(mask_row[None, None, :], scores, -1e30)


def attend_forward(query_rows, key_rows, value_rows, key_valid, head_count):
    image_count = key_valid.shape[0]

    def one_image(image_items):
        query_img, key_img, value_img, mask_row = image_items
        scores = masked_scores(query_img, key_img, mask_row)
        row_peak = jnp.max(scores, axis=-1, keepdims=True)
        exponent = jnp.exp(scores - row_peak)
        row_total = jnp.sum(exponent, axis=-1, keepdims=True)
        attn_probs = (exponent / row_total).astype(jnp.bfloat16)
        head_mixed = jnp.einsum(
            "hqk,khd->qhd", attn_probs, value_img, preferred_element_type=jnp.float32
        )
        return (head_mixed.astype(jnp.bfloat16), (row_peak + jnp.log(row_total))[:, :, 0])

    head_mixed, log_total = lax.map(
        one_image,
        (
            split_heads(query_rows, image_count, head_count),
            split_heads(key_rows, image_count, head_count),
            split_heads(value_rows, image_count, head_count),
            key_valid,
        ),
    )
    return (head_mixed.reshape(query_rows.shape), log_total)


def attend_backward(query_rows, key_rows, value_rows, grad_rows, log_total, key_valid, head_count):
    image_count = key_valid.shape[0]
    scale = HEAD_DIM ** (-0.5)

    def one_image(image_items):
        query_img, key_img, value_img, grad_img, total_img, mask_row = image_items
        scores = masked_scores(query_img, key_img, mask_row)
        attn_probs = jnp.exp(scores - total_img[:, :, None])
        grad_probs = jnp.einsum(
            "qhd,khd->hqk", grad_img, value_img, preferred_element_type=jnp.float32
        )
        grad_values = jnp.einsum(
            "hqk,qhd->khd",
            attn_probs.astype(jnp.bfloat16),
            grad_img,
            preferred_element_type=jnp.float32,
        ).astype(jnp.bfloat16)
        inner = jnp.sum(attn_probs * grad_probs, axis=-1, keepdims=True)
        grad_scores = (attn_probs * (grad_probs - inner)).astype(jnp.bfloat16)
        grad_queries = (
            jnp.einsum("hqk,khd->qhd", grad_scores, key_img, preferred_element_type=jnp.float32)
            * scale
        ).astype(jnp.bfloat16)
        grad_keys = (
            jnp.einsum("hqk,qhd->khd", grad_scores, query_img, preferred_element_type=jnp.float32)
            * scale
        ).astype(jnp.bfloat16)
        return (grad_queries, grad_keys, grad_values)

    grad_queries, grad_keys, grad_values = lax.map(
        one_image,
        (
            split_heads(query_rows, image_count, head_count),
            split_heads(key_rows, image_count, head_count),
            split_heads(value_rows, image_count, head_count),
            split_heads(grad_rows, image_count, head_count),
            log_total,
            key_valid,
        ),
    )
    return (
        grad_queries.reshape(query_rows.shape),
        grad_keys.reshape(query_rows.shape),
        grad_values.reshape(query_rows.shape),
    )


def forward_block(resid, key_valid, weights):
    (
        norm_gains,
        shifts,
        project_in,
        project_bias,
        project_out,
        out_bias,
        scales,
        up_weight,
        up_bias,
        down_weight,
    ) = weights
    head_count = project_in.shape[2] // HEAD_DIM
    normed_rows = gather_rows(layer_norm(resid, norm_gains[0], shifts[0]).astype(jnp.bfloat16))
    query_rows = (matmul(normed_rows, project_in[0]) + project_bias[0]).astype(jnp.bfloat16)
    key_rows = matmul(normed_rows, project_in[1]).astype(jnp.bfloat16)
    value_rows = (matmul(normed_rows, project_in[2]) + project_bias[1]).astype(jnp.bfloat16)
    head_mixed, log_total = attend_forward(query_rows, key_rows, value_rows, key_valid, head_count)
    attn_out = branch_rows(head_mixed, project_out) + out_bias[0]
    middle = resid + scales[0] * attn_out
    mlp_rows = gather_rows(layer_norm(middle, norm_gains[1], shifts[1]).astype(jnp.bfloat16))
    pre_act = matmul(mlp_rows, up_weight) + up_bias
    hidden = gelu_exact(pre_act).astype(jnp.bfloat16)
    mlp_out = branch_rows(hidden, down_weight) + out_bias[1]
    result = middle + scales[1] * mlp_out
    kept = (
        resid,
        normed_rows,
        query_rows,
        key_rows,
        value_rows,
        head_mixed,
        log_total,
        attn_out,
        middle,
        mlp_rows,
        pre_act,
        hidden,
        mlp_out,
    )
    return (result, kept)


def backward_block(grad_out, key_valid, weights, kept):
    (
        norm_gains,
        shifts,
        project_in,
        project_bias,
        project_out,
        out_bias,
        scales,
        up_weight,
        up_bias,
        down_weight,
    ) = weights
    (
        resid,
        normed_rows,
        query_rows,
        key_rows,
        value_rows,
        head_mixed,
        log_total,
        attn_out,
        middle,
        mlp_rows,
        pre_act,
        hidden,
        mlp_out,
    ) = kept
    local_rows = grad_out.shape[0]
    head_count = project_in.shape[2] // HEAD_DIM
    scale_mlp = jnp.sum(grad_out * mlp_out, axis=0)
    grad_branch = (scales[1] * grad_out).astype(jnp.bfloat16)
    bias_mlp = column_sums(grad_branch)
    branch_all = gather_grads(grad_branch)
    grad_hidden = matmul_nt(branch_all, down_weight)
    grad_down = matmul_tn(hidden, branch_all)
    gelu_value, gelu_back = jax.vjp(gelu_exact, pre_act)
    grad_pre = gelu_back(grad_hidden)[0].astype(jnp.bfloat16)
    grad_up_bias = column_sums(grad_pre)
    grad_up = matmul_tn(mlp_rows, grad_pre)
    grad_normed_mlp = input_rows((grad_pre,), (up_weight,), local_rows)
    norm_value, norm_back = jax.vjp(layer_norm, middle, norm_gains[1], shifts[1])
    grad_middle, gain_mlp, shift_mlp = norm_back(grad_normed_mlp)
    grad_middle = grad_out + grad_middle
    scale_attn = jnp.sum(grad_middle * attn_out, axis=0)
    grad_attn = (scales[0] * grad_middle).astype(jnp.bfloat16)
    bias_attn = column_sums(grad_attn)
    attn_all = gather_grads(grad_attn)
    grad_mixed = matmul_nt(attn_all, project_out).astype(jnp.bfloat16)
    grad_out_proj = matmul_tn(head_mixed, attn_all)
    grad_queries, grad_keys, grad_values = attend_backward(
        query_rows, key_rows, value_rows, grad_mixed, log_total, key_valid, head_count
    )
    grad_in_proj = jnp.stack(
        [
            matmul_tn(normed_rows, grad_queries),
            matmul_tn(normed_rows, grad_keys),
            matmul_tn(normed_rows, grad_values),
        ]
    )
    grad_in_bias = jnp.stack([column_sums(grad_queries), column_sums(grad_values)])
    grad_normed = input_rows(
        (grad_queries, grad_keys, grad_values),
        (project_in[0], project_in[1], project_in[2]),
        local_rows,
    )
    first_value, first_back = jax.vjp(layer_norm, resid, norm_gains[0], shifts[0])
    grad_resid, gain_attn, shift_attn = first_back(grad_normed)
    grad_resid = grad_middle + grad_resid
    larger = (grad_in_proj, grad_in_bias, grad_out_proj, grad_up, grad_up_bias, grad_down)
    smaller = (
        jnp.stack([gain_attn, gain_mlp]),
        jnp.stack([shift_attn, shift_mlp]),
        jnp.stack([bias_attn, bias_mlp]),
        jnp.stack([scale_attn, scale_mlp]),
    )
    return (grad_resid, larger, smaller)


def arrange(larger, smaller):
    return (
        smaller[0],
        smaller[1],
        larger[0],
        larger[1],
        larger[2],
        smaller[2],
        smaller[3],
        larger[3],
        larger[4],
        larger[5],
    )


def body(
    inputs,
    lengths,
    cotangent,
    student_gains,
    student_shifts,
    student_project_in,
    student_project_bias,
    student_project_out,
    student_out_bias,
    student_scales,
    student_up_weight,
    student_up_bias,
    student_down_weight,
    teacher_gains,
    teacher_shifts,
    teacher_project_in,
    teacher_project_bias,
    teacher_project_out,
    teacher_out_bias,
    teacher_scales,
    teacher_up_weight,
    teacher_up_bias,
    teacher_down_weight,
):
    student = (
        student_gains,
        student_shifts,
        student_project_in,
        student_project_bias,
        student_project_out,
        student_out_bias,
        student_scales,
        student_up_weight,
        student_up_bias,
        student_down_weight,
    )
    teacher = (
        teacher_gains,
        teacher_shifts,
        teacher_project_in,
        teacher_project_bias,
        teacher_project_out,
        teacher_out_bias,
        teacher_scales,
        teacher_up_weight,
        teacher_up_bias,
        teacher_down_weight,
    )
    key_valid = lax.broadcasted_iota(jnp.int32, (lengths.shape[0], SLOT), 1) < lengths[:, None]
    start_rows = inputs.astype(jnp.float32)
    student_out, student_kept = forward_block(start_rows, key_valid, student)
    teacher_out, teacher_kept = forward_block(student_out, key_valid, teacher)
    grad_mid, teacher_large, teacher_small = backward_block(
        cotangent.astype(jnp.float32), key_valid, teacher, teacher_kept
    )
    again_out, student_kept = forward_block(start_rows, key_valid, student)
    grad_input, student_large, student_small = backward_block(
        grad_mid, key_valid, student, student_kept
    )
    summed = lax.psum(
        (
            teacher_large[0],
            teacher_large[1],
            teacher_large[2],
            teacher_large[3],
            teacher_large[4],
            teacher_large[5],
            student_large[0],
            student_large[1],
            student_large[2],
            student_large[3],
            student_large[4],
            student_large[5],
        ),
        "dp",
    )
    small_summed = lax.psum(
        (
            teacher_small[0],
            teacher_small[1],
            teacher_small[2],
            teacher_small[3],
            student_small[0],
            student_small[1],
            student_small[2],
            student_small[3],
        ),
        ("dp", "mp"),
    )
    teacher_large = summed[:6]
    student_large = summed[6:]
    teacher_small = small_summed[:4]
    student_small = small_summed[4:]
    return (
        (teacher_out.astype(jnp.bfloat16), grad_input.astype(jnp.bfloat16))
        + arrange(student_large, student_small)
        + arrange(teacher_large, teacher_small)
    )


def solution(mesh):
    in_specs = (
        P(("dp", "mp"), None),
        P("dp"),
        P(("dp", "mp"), None),
        P(),
        P(),
        P(None, None, "mp"),
        P(None, "mp"),
        P("mp", None),
        P(),
        P(),
        P(None, "mp"),
        P("mp"),
        P("mp", None),
        P(),
        P(),
        P(None, None, "mp"),
        P(None, "mp"),
        P("mp", None),
        P(),
        P(),
        P(None, "mp"),
        P("mp"),
        P("mp", None),
    )
    out_specs = (
        P(("dp", "mp"), None),
        P(("dp", "mp"), None),
        P(),
        P(),
        P(None, None, "mp"),
        P(None, "mp"),
        P("mp", None),
        P(),
        P(),
        P(None, "mp"),
        P("mp"),
        P("mp", None),
        P(),
        P(),
        P(None, None, "mp"),
        P(None, "mp"),
        P("mp", None),
        P(),
        P(),
        P(None, "mp"),
        P("mp"),
        P("mp", None),
    )
    return jax.shard_map(body, mesh=mesh, in_specs=in_specs, out_specs=out_specs, check_vma=False)
```

profile of v0, /device:TPU:0, one launch (start us, length us, event | category | flops | bytes accessed | tf_op | source)
XLA Modules:
  0.0 1247.9 jit_solution(6753274581541259221)
XLA Ops:
  15.5 44.9 %all-gather.10.cloned.1.call-done = bf16[1280,768]{1,0:T(8,128)(2,1)} async-done(((bf16[320,768]{1,0:T(8,128)(2,1)}), bf16[1280,768]{1,0:T(8,128)(2,1)}) %all-gather.10.cloned.1.call-update) | async-done | bytes 1966096 | tf_op jit(solution)/shard_map/all_gather | solution.py:44
  60.3 3.3 fusion.182
  78.3 16.1 %while.62 = (s32[]{:T(128)}, bf16[2,640,3,64]{1,3,2,0:T(8,128)(2,1)S(1)}, bf16[2,640,3,64]{1,3,2,0:T(8,128)(2,1)}, pred[2,640]{1,0:T(4,128)(4,1)S(1)}, bf16[2,64...) while((s32[]{:T(128)}, bf16[2,640,3,64]{1,3,2,0:T(8,128)(2,1)S(1)}, ...), condition=%wide.region_5.6_spmd, body=%wide.region_2.5_spmd.sunk | while | flops 322069120 | bytes 12801525 | solution.py:92
  78.4 5.0 fusion.408
  86.4 5.0 fusion.408
  97.1 9.5 while.65
  110.5 27.0 %reduce-scatter.11.cloned.1.call-done = bf16[320,768]{1,0:T(8,128)(2,1)} async-done(((bf16[1280,768]{1,0:T(8,128)(2,1)}), bf16[320,768]{1,0:T(8,128)(2,1)}) %reduce-scatter.11.cloned.1.call-update) | async-done | bytes 491536 | tf_op jit(solution)/shard_map/reduce_scatter | solution.py:52
  137.5 43.6 %reduce-scatter.23.cloned.1.call-done = bf16[320,768]{1,0:T(8,128)(2,1)} async-done(((bf16[1280,768]{1,0:T(8,128)(2,1)}), bf16[320,768]{1,0:T(8,128)(2,1)}) %reduce-scatter.23.cloned.1.call-update) | async-done | bytes 491536 | tf_op jit(solution)/shard_map/reduce_scatter | solution.py:52
  187.6 42.9 %all-gather.12.cloned.1.call-done = bf16[1280,768]{1,0:T(8,128)(2,1)} async-done(((bf16[320,768]{1,0:T(8,128)(2,1)}), bf16[1280,768]{1,0:T(8,128)(2,1)}) %all-gather.12.cloned.1.call-update) | async-done | bytes 1966096 | tf_op jit(solution)/shard_map/all_gather | solution.py:44
  230.4 14.0 %convolution_convert_fusion.7 = bf16[1280,768]{1,0:T(8,128)(2,1)} fusion(bf16[768,768]{1,0:T(8,128)(2,1)S(1)} %copy-done, bf16[1280,768]{1,0:T(8,128)(2,1)} %all-gather.12.cloned.1.call-done, bf16[768,768]{1,0:T(8,128)(2,1)} %param.43, f32[768]{0:T(1024)S(1)} %copy-done.128), kind=kOutput, calls=%fused_computation.228 | convolution fusion | flops 3085762560 | bytes 6294528 | tf_op jit(solution)/shard_map/dot_general | solution.py:24
  244.6 40.3 %reduce-scatter.13.cloned.1.call-done = bf16[320,768]{1,0:T(8,128)(2,1)} async-done(((bf16[1280,768]{1,0:T(8,128)(2,1)}), bf16[320,768]{1,0:T(8,128)(2,1)}) %reduce-scatter.13.cloned.1.call-update) | async-done | bytes 491536 | tf_op jit(solution)/shard_map/reduce_scatter | solution.py:52
  288.2 42.5 %all-gather.14.cloned.1.call-done = bf16[1280,768]{1,0:T(8,128)(2,1)} async-done(((bf16[320,768]{1,0:T(8,128)(2,1)}), bf16[1280,768]{1,0:T(8,128)(2,1)}) %all-gather.14.cloned.1.call-update) | async-done | bytes 1966096 | tf_op jit(solution)/shard_map/all_gather | solution.py:44
  333.2 3.1 fusion.183
  343.5 8.9 while.63
  357.0 40.3 %reduce-scatter.15.cloned.1.call-done = bf16[320,768]{1,0:T(8,128)(2,1)} async-done(((bf16[1280,768]{1,0:T(8,128)(2,1)}), bf16[320,768]{1,0:T(8,128)(2,1)}) %reduce-scatter.15.cloned.1.call-update) | async-done | bytes 491536 | tf_op jit(solution)/shard_map/reduce_scatter | solution.py:52
  403.4 40.1 %all-gather.16.cloned.1.call-done = bf16[1280,768]{1,0:T(8,128)(2,1)} async-done(((bf16[320,768]{1,0:T(8,128)(2,1)}), bf16[1280,768]{1,0:T(8,128)(2,1)}) %all-gather.16.cloned.1.call-update) | async-done | bytes 1966096 | tf_op jit(solution)/shard_map/all_gather | solution.py:44
  443.6 5.6 convolution_add_fusion.5
  449.1 39.0 %all-gather.18.cloned.1.call-done = bf16[1280,768]{1,0:T(8,128)(2,1)} async-done(((bf16[320,768]{1,0:T(8,128)(2,1)}), bf16[1280,768]{1,0:T(8,128)(2,1)}) %all-gather.18.cloned.1.call-update) | async-done | bytes 1966096 | tf_op jit(solution)/shard_map/all_gather | solution.py:48
  488.1 14.0 %convert_reduce_fusion = (f32[768]{0:T(1024)}, bf16[1280,768]{1,0:T(8,128)(2,1)S(1)}, f32[1280,768]{1,0:T(8,128)}) fusion(f32[1280,768]{1,0:T(8,128)} %convolution_add_fusion.5, bf16[1280,768]{1,0:T(8,128)(2,1)} %all-gather.18.cloned.1.call-done, bf16[768,768]{1,0:T(8,128)(2,1)} %param.55), kind=kOutput, calls=%fused_computation.170 | convolution fusion | flops 1582693632 | bytes 12979200 | tf_op jit(solution)/shard_map/dot_general | solution.py:34
  503.4 3.0 convolution_convert_fusion.5
  506.5 3.9 multiply_convert_fusion.3
  514.9 32.0 %reduce-scatter.19.cloned.1.call-done = bf16[320,768]{1,0:T(8,128)(2,1)} async-done(((bf16[1280,768]{1,0:T(8,128)(2,1)}), bf16[320,768]{1,0:T(8,128)(2,1)}) %reduce-scatter.19.cloned.1.call-update) | async-done | bytes 491536 | tf_op jit(solution)/shard_map/reduce_scatter | solution.py:61
  549.3 41.2 %reduce-scatter.17.cloned.1.call-done = bf16[320,768]{1,0:T(8,128)(2,1)} async-done(((bf16[1280,768]{1,0:T(8,128)(2,1)}), bf16[320,768]{1,0:T(8,128)(2,1)}) %reduce-scatter.17.cloned.1.call-update) | async-done | bytes 491536 | tf_op jit(solution)/shard_map/reduce_scatter | solution.py:52
  594.2 3.2 multiply_reduce_fusion.2
  597.6 42.7 %all-gather.20.cloned.1.call-done = bf16[1280,768]{1,0:T(8,128)(2,1)} async-done(((bf16[320,768]{1,0:T(8,128)(2,1)}), bf16[1280,768]{1,0:T(8,128)(2,1)}) %all-gather.20.cloned.1.call-update) | async-done | bytes 1966096 | tf_op jit(solution)/shard_map/all_gather | solution.py:48
  640.3 3.1 convolution_convert_fusion.9
  649.7 16.5 %while.64 = (s32[]{:T(128)}, bf16[2,640,3,64]{1,3,2,0:T(8,128)(2,1)}, bf16[2,640,3,64]{1,3,2,0:T(8,128)(2,1)}, bf16[2,640,3,64]{1,3,2,0:T(8,128)(2,1)}, bf16[2,6...) while((s32[]{:T(128)}, ...), condition=%wide.region_25.26_spmd, body=%wide.region_23.25_spmd.sunk | while | flops 805476480 | bytes 55118556 | solution.py:133
  675.0 39.4 %reduce-scatter.21.cloned.1.call-done = bf16[320,768]{1,0:T(8,128)(2,1)} async-done(((bf16[1280,768]{1,0:T(8,128)(2,1)}), bf16[320,768]{1,0:T(8,128)(2,1)}) %reduce-scatter.21.cloned.1.call-update) | async-done | bytes 491536 | tf_op jit(solution)/shard_map/reduce_scatter | solution.py:61
  718.6 3.4 convert_reduce_fusion.11
  722.1 37.1 %all-gather.22.cloned.1.call-done = bf16[1280,768]{1,0:T(8,128)(2,1)} async-done(((bf16[320,768]{1,0:T(8,128)(2,1)}), bf16[1280,768]{1,0:T(8,128)(2,1)}) %all-gather.22.cloned.1.call-update) | async-done | bytes 1966096 | tf_op jit(solution)/shard_map/all_gather | solution.py:44
  759.2 5.5 convolution_add_fusion.4
  764.7 38.9 %all-gather.24.cloned.1.call-done = bf16[1280,768]{1,0:T(8,128)(2,1)} async-done(((bf16[320,768]{1,0:T(8,128)(2,1)}), bf16[1280,768]{1,0:T(8,128)(2,1)}) %all-gather.24.cloned.1.call-update) | async-done | bytes 1966096 | tf_op jit(solution)/shard_map/all_gather | solution.py:48
  803.6 13.0 %convert_reduce_fusion.1 = (f32[768]{0:T(1024)S(1)}, bf16[1280,768]{1,0:T(8,128)(2,1)S(1)}, f32[1280,768]{1,0:T(8,128)}) fusion(f32[1280,768]{1,0:T(8,128)} %convolution_add_fusion.4, bf16[1280,768]{1,0:T(8,128)(2,1)} %all-gather.24.cloned.1.call-done, bf16[768,768]{1,0:T(8,128)(2,1)S(1)} %copy-done), kind=kOutput, calls=%fused_computation.171 | convolution fusion | flops 1582693632 | bytes 12979200 | tf_op jit(solution)/shard_map/dot_general | solution.py:34
  817.9 3.0 convolution_convert_fusion.4
  821.0 3.9 multiply_convert_fusion.2
  826.2 3.0 convolution_convert_fusion.3
  829.3 32.1 %reduce-scatter.25.cloned.1.call-done = bf16[320,768]{1,0:T(8,128)(2,1)} async-done(((bf16[1280,768]{1,0:T(8,128)(2,1)}), bf16[320,768]{1,0:T(8,128)(2,1)}) %reduce-scatter.25.cloned.1.call-update) | async-done | bytes 491536 | tf_op jit(solution)/shard_map/reduce_scatter | solution.py:61
  864.9 40.0 %reduce-scatter.29.cloned.1.call-done = bf16[320,768]{1,0:T(8,128)(2,1)} async-done(((bf16[1280,768]{1,0:T(8,128)(2,1)}), bf16[320,768]{1,0:T(8,128)(2,1)}) %reduce-scatter.29.cloned.1.call-update) | async-done | bytes 491536 | tf_op jit(solution)/shard_map/reduce_scatter | solution.py:52
  908.2 42.7 %all-gather.26.cloned.1.call-done = bf16[1280,768]{1,0:T(8,128)(2,1)} async-done(((bf16[320,768]{1,0:T(8,128)(2,1)}), bf16[1280,768]{1,0:T(8,128)(2,1)}) %all-gather.26.cloned.1.call-update) | async-done | bytes 1966096 | tf_op jit(solution)/shard_map/all_gather | solution.py:48
  950.9 3.1 convolution_convert_fusion.8
  960.3 21.9 %while.66 = (s32[]{:T(128)}, bf16[2,640,3,64]{1,3,2,0:T(8,128)(2,1)}, bf16[2,640,3,64]{1,3,2,0:T(8,128)(2,1)}, bf16[2,640,3,64]{1,3,2,0:T(8,128)(2,1)}, bf16[2,6...) while((s32[]{:T(128)}, ...), condition=%wide.region_41.42_spmd, body=%wide.region_39.41_spmd.sunk | while | flops 805476480 | bytes 53152448 | solution.py:133
  990.0 5.4 fusion.298
  995.5 3.2 fusion.297
  1003.6 3.2 fusion.295
  1006.8 3.2 fusion.294
  1019.5 24.5 %all-reduce.1 = (f32[2,192]{1,0:T(2,128)}, f32[768]{0:T(1024)}, f32[2,192]{1,0:T(2,128)}, f32[768]{0:T(1024)}) all-reduce(f32[2,192]{1,0:T(2,128)S(1)} %pad_maximum_fusion.10, f32[768]{0:T(1024)S(1)} %get-tuple-element.469, f32[2,192]{1,0:T(2,128)S(1)} %pad_maximum_fusion.11, ...), channel_id=1, replica_groups=mesh['dp'=8,'mp'=4] {'dp'}, use_global_device_ids=true, to_apply=%region_54.55 | all-reduce | flops 2304 | bytes 18432 | tf_op jit(solution)/shard_map/psum | solution.py:349
  1047.2 40.8 %all-reduce = (f32[2,768]{1,0:T(2,128)}, f32[2,768]{1,0:T(2,128)}, f32[2,768]{1,0:T(2,128)}, f32[2,768]{1,0:T(2,128)}, f32[2,768]{1,0:T(2,128)}, /*index=5*/f32[...) all-reduce(f32[2,768]{1,0:T(2,128)S(1)} %pad_maximum_fusion.2, ...), channel_id=1, replica_groups=mesh['dp'=8,'mp'=4] {'dp','mp'}, use_global_device_ids=true, to_apply=%region_47.48 | all-reduce | flops 12288 | bytes 98304 | tf_op jit(solution)/shard_map/psum | solution.py:366
  1090.2 139.0 %all-reduce.5.cloned.1.call-done = (f32[3,768,192]{1,2,0:T(8,128)}, f32[192,768]{1,0:T(8,128)}, f32[768,768]{1,0:T(8,128)}, f32[768,768]{1,0:T(8,128)}, f32[3,76...) async-done(((f32[3,768,192]{1,2,0:T(8,128)}, f32[192,768]{1,0:T(8,128)}, f32[768,768]{1,0:T(8,128)}, f32[768,768]{1,0:T(8,128)}, ...) | async-done | bytes 14155792 | tf_op jit(solution)/shard_map/psum | solution.py:349
  (555 shorter events, 206.7 us)
Async XLA Ops:
  7.2 223.3 %copy-start = (bf16[768,768]{1,0:T(8,128)(2,1)S(1)}, bf16[768,768]{1,0:T(8,128)(2,1)}, u32[]{:S(2)}) copy-start(bf16[768,768]{1,0:T(8,128)(2,1)} %param.45) | copy-start | bytes 3538948
  7.2 53.1 %all-gather.10.cloned.1.call-start = ((), (), s32[]{:S(2)}) async-start(), calls=%async_computation.10 | async-start | bytes 2457600 | tf_op jit(solution)/shard_map/all_gather | solution.py:44
  11.3 173.4 %copy-start.83 = (f32[768]{0:T(1024)}, f32[768]{0:T(1024)S(1)}, u32[]{:S(2)}) copy-start(f32[768]{0:T(1024)S(1)} %get-tuple-element.509) | copy-start | bytes 9220
  13.9 123.5 %reduce-scatter.11.cloned.1.call-start = ((), (), s32[]{:S(2)}) async-start(), calls=%async_computation.11 | async-start | bytes 2457600 | tf_op jit(solution)/shard_map/reduce_scatter | solution.py:52
  97.0 84.0 %reduce-scatter.23.cloned.1.call-start = ((), (), s32[]{:S(2)}) async-start(), calls=%async_computation.22 | async-start | bytes 2457600 | tf_op jit(solution)/shard_map/reduce_scatter | solution.py:52
  106.7 76.1 %copy-start.77 = (f32[2,3,640]{2,1,0:T(4,128)}, f32[2,3,640]{2,1,0:T(4,128)S(1)}, u32[]{:S(2)}) copy-start(f32[2,3,640]{2,1,0:T(4,128)S(1)} %get-tuple-element.891) | copy-start | bytes 46084
  106.7 74.4 %copy-start.1 = (bf16[320,768]{1,0:T(8,128)(2,1)S(1)}, bf16[320,768]{1,0:T(8,128)(2,1)}, u32[]{:S(2)}) copy-start(bf16[320,768]{1,0:T(8,128)(2,1)} %param.33) | copy-start | bytes 1474564
  110.1 120.4 %copy-start.128 = (f32[768]{0:T(1024)S(1)}, f32[768]{0:T(1024)}, u32[]{:S(2)}) copy-start(f32[768]{0:T(1024)} %param.44) | copy-start | bytes 9220
  110.1 120.3 %all-gather.12.cloned.1.call-start = ((), (), s32[]{:S(2)}) async-start(), calls=%async_computation.12 | async-start | bytes 2457600 | tf_op jit(solution)/shard_map/all_gather | solution.py:44
  110.4 174.5 %copy-start.72 = (f32[768]{0:T(1024)}, f32[768]{0:T(1024)S(1)}, u32[]{:S(2)}) copy-start(f32[768]{0:T(1024)S(1)} %get-tuple-element.511) | copy-start | bytes 9220
  110.4 174.5 %copy-start.75 = (f32[768]{0:T(1024)}, f32[768]{0:T(1024)S(1)}, u32[]{:S(2)}) copy-start(f32[768]{0:T(1024)S(1)} %get-tuple-element.361) | copy-start | bytes 9220
  110.4 174.5 %copy-start.91 = (f32[768]{0:T(1024)}, f32[768]{0:T(1024)S(1)}, u32[]{:S(2)}) copy-start(f32[768]{0:T(1024)S(1)} %get-tuple-element.512) | copy-start | bytes 9220
  110.5 174.4 %copy-start.93 = (f32[768]{0:T(1024)}, f32[768]{0:T(1024)S(1)}, u32[]{:S(2)}) copy-start(f32[768]{0:T(1024)S(1)} %get-tuple-element.360) | copy-start | bytes 9220
  187.5 57.0 %copy-start.118 = (f32[2,768]{1,0:T(2,128)S(1)}, f32[2,768]{1,0:T(2,128)}, u32[]{:S(2)}) copy-start(f32[2,768]{1,0:T(2,128)} %param.47) | copy-start | bytes 18436
  187.5 57.0 %copy-start.119 = (f32[2,768]{1,0:T(2,128)S(1)}, f32[2,768]{1,0:T(2,128)}, u32[]{:S(2)}) copy-start(f32[2,768]{1,0:T(2,128)} %param.46) | copy-start | bytes 18436
  187.5 97.4 %copy-start.13 = (bf16[320,768]{1,0:T(8,128)(2,1)S(1)}, bf16[320,768]{1,0:T(8,128)(2,1)}, u32[]{:S(2)}) copy-start(bf16[320,768]{1,0:T(8,128)(2,1)} %reduce-scatter.11.cloned.1.call-done) | copy-start | bytes 1474564
  187.5 97.4 %reduce-scatter.13.cloned.1.call-start = ((), (), s32[]{:S(2)}) async-start(), calls=%async_computation.13 | async-start | bytes 2457600 | tf_op jit(solution)/shard_map/reduce_scatter | solution.py:52
  244.4 43.7 %copy-start.123 = (f32[2,192]{1,0:T(2,128)S(1)}, f32[2,192]{1,0:T(2,128)}, u32[]{:S(2)}) copy-start(f32[2,192]{1,0:T(2,128)} %param.49) | copy-start | bytes 4612
  244.5 86.2 %all-gather.14.cloned.1.call-start = ((), (), s32[]{:S(2)}) async-start(), calls=%async_computation.14 | async-start | bytes 2457600 | tf_op jit(solution)/shard_map/all_gather | solution.py:44
  244.6 88.4 %copy-start.81 = (f32[768]{0:T(1024)}, f32[768]{0:T(1024)S(1)}, u32[]{:S(2)}) copy-start(f32[768]{0:T(1024)S(1)} %get-tuple-element.513) | copy-start | bytes 9220
  286.4 46.8 %copy-start.89 = (f32[320]{0:T(512)}, f32[320]{0:T(512)S(1)}, u32[]{:S(2)}) copy-start(f32[320]{0:T(512)S(1)} %broadcast_multiply_fusion.2) | copy-start | bytes 3844
  286.6 49.7 %copy-start.105 = (f32[320]{0:T(512)}, f32[320]{0:T(512)S(1)}, u32[]{:S(2)}) copy-start(f32[320]{0:T(512)S(1)} %multiply_reduce_fusion.7) | copy-start | bytes 3844
  286.7 49.7 %copy-start.99 = (f32[320]{0:T(512)}, f32[320]{0:T(512)S(1)}, u32[]{:S(2)}) copy-start(f32[320]{0:T(512)S(1)} %fusion.241) | copy-start | bytes 3844
  287.7 109.6 %reduce-scatter.15.cloned.1.call-start = ((), (), s32[]{:S(2)}) async-start(), calls=%async_computation.15 | async-start | bytes 2457600 | tf_op jit(solution)/shard_map/reduce_scatter | solution.py:52
  356.9 86.6 %copy-start.127 = (f32[768]{0:T(1024)S(1)}, f32[768]{0:T(1024)}, u32[]{:S(2)}) copy-start(f32[768]{0:T(1024)} %param.54) | copy-start | bytes 9220
  356.9 86.6 %all-gather.16.cloned.1.call-start = ((), (), s32[]{:S(2)}) async-start(), calls=%async_computation.16 | async-start | bytes 2457600 | tf_op jit(solution)/shard_map/all_gather | solution.py:44
  400.6 87.5 %all-gather.18.cloned.1.call-start = ((), (), s32[]{:S(2)}) async-start(), calls=%async_computation.18 | async-start | bytes 2457600 | tf_op jit(solution)/shard_map/all_gather | solution.py:48
  403.2 143.7 %reduce-scatter.19.cloned.1.call-start = ((), (), s32[]{:S(2)}) async-start(), calls=%async_computation.19 | async-start | bytes 2457600 | tf_op jit(solution)/shard_map/reduce_scatter | solution.py:61
  506.5 84.0 %reduce-scatter.17.cloned.1.call-start = ((), (), s32[]{:S(2)}) async-start(), calls=%async_computation.17 | async-start | bytes 2457600 | tf_op jit(solution)/shard_map/reduce_scatter | solution.py:52
  514.9 125.4 %all-gather.20.cloned.1.call-start = ((), (), s32[]{:S(2)}) async-start(), calls=%async_computation.20 | async-start | bytes 2457600 | tf_op jit(solution)/shard_map/all_gather | solution.py:48
  597.4 117.0 %reduce-scatter.21.cloned.1.call-start = ((), (), s32[]{:S(2)}) async-start(), calls=%async_computation.21 | async-start | bytes 2457600 | tf_op jit(solution)/shard_map/reduce_scatter | solution.py:61
  671.9 44.5 %copy-start.106 = (f32[320]{0:T(512)S(1)}, f32[320]{0:T(512)}, u32[]{:S(2)}) copy-start(f32[320]{0:T(512)} %copy-done.105) | copy-start | bytes 3844
  671.9 44.5 %copy-start.100 = (f32[320]{0:T(512)S(1)}, f32[320]{0:T(512)}, u32[]{:S(2)}) copy-start(f32[320]{0:T(512)} %copy-done.99) | copy-start | bytes 3844
  673.9 44.7 %copy-start.9 = (f32[320,768]{1,0:T(8,128)S(1)}, f32[320,768]{1,0:T(8,128)}, u32[]{:S(2)}) copy-start(f32[320,768]{1,0:T(8,128)} %copy-done.8) | copy-start | bytes 2949124
  673.9 44.7 %copy-start.92 = (f32[768]{0:T(1024)S(1)}, f32[768]{0:T(1024)}, u32[]{:S(2)}) copy-start(f32[768]{0:T(1024)} %copy-done.91) | copy-start | bytes 9220
  673.9 85.3 %all-gather.22.cloned.1.call-start = ((), (), s32[]{:S(2)}) async-start(), calls=%async_computation.23 | async-start | bytes 2457600 | tf_op jit(solution)/shard_map/all_gather | solution.py:44
  674.5 84.7 %copy-start.129 = (f32[768]{0:T(1024)S(1)}, f32[768]{0:T(1024)}, u32[]{:S(2)}) copy-start(f32[768]{0:T(1024)} %param.44) | copy-start | bytes 9220
  674.5 129.1 %all-gather.24.cloned.1.call-start = ((), (), s32[]{:S(2)}) async-start(), calls=%async_computation.24 | async-start | bytes 2457600 | tf_op jit(solution)/shard_map/all_gather | solution.py:48
  722.0 139.4 %reduce-scatter.25.cloned.1.call-start = ((), (), s32[]{:S(2)}) async-start(), calls=%async_computation.25 | async-start | bytes 2457600 | tf_op jit(solution)/shard_map/reduce_scatter | solution.py:61
  764.7 53.2 %copy-start.126 = (bf16[768,768]{1,0:T(8,128)(2,1)S(1)}, bf16[768,768]{1,0:T(8,128)(2,1)}, u32[]{:S(2)}) copy-start(bf16[768,768]{1,0:T(8,128)(2,1)} %param.43) | copy-start | bytes 3538948
  821.0 83.9 %reduce-scatter.29.cloned.1.call-start = ((), (), s32[]{:S(2)}) async-start(), calls=%async_computation.28 | async-start | bytes 2457600 | tf_op jit(solution)/shard_map/reduce_scatter | solution.py:52
  829.2 75.6 %copy-start.94 = (f32[768]{0:T(1024)S(1)}, f32[768]{0:T(1024)}, u32[]{:S(2)}) copy-start(f32[768]{0:T(1024)} %copy-done.93) | copy-start | bytes 9220
  829.3 121.6 %all-gather.26.cloned.1.call-start = ((), (), s32[]{:S(2)}) async-start(), calls=%async_computation.26 | async-start | bytes 2457600 | tf_op jit(solution)/shard_map/all_gather | solution.py:48
  863.0 87.9 %copy-start.67 = (bf16[192,768]{1,0:T(8,128)(2,1)S(1)}, bf16[192,768]{1,0:T(8,128)(2,1)}, u32[]{:S(2)}) copy-start(bf16[192,768]{1,0:T(8,128)(2,1)} %param.40) | copy-start | bytes 884740
  907.0 53.3 %copy-start.16 = (bf16[2,640,3,64]{1,3,2,0:T(8,128)(2,1)S(1)}, bf16[2,640,3,64]{1,3,2,0:T(8,128)(2,1)}, u32[]{:S(2)}) copy-start(bf16[2,640,3,64]{1,3,2,0:T(8,128)(2,1)} %get-tuple-element.997) | copy-start | bytes 1474564
  907.0 53.3 %copy-start.78 = (f32[2,3,640]{2,1,0:T(4,128)S(1)}, f32[2,3,640]{2,1,0:T(4,128)}, u32[]{:S(2)}) copy-start(f32[2,3,640]{2,1,0:T(4,128)} %copy-done.77) | copy-start | bytes 46084
  907.9 136.1 %reduce-scatter.27.cloned.1.call-start = ((), (), s32[]{:S(2)}) async-start(), calls=%async_computation.27 | async-start | bytes 2457600 | tf_op jit(solution)/shard_map/reduce_scatter | solution.py:61
  989.7 239.5 %all-reduce.5.cloned.1.call-start = ((), (), s32[]{:S(2)}) async-start(), calls=%async_computation.29 | async-start | bytes 28311552 | tf_op jit(solution)/shard_map/psum | solution.py:349
  (121 other events, 785.0 us)
Sparse Core Ops, SparseCore 0:
  14.0 46.2 all-gather.9
  97.1 40.2 reduce-scatter.10
  140.4 40.6 reduce-scatter.22
  187.6 42.8 all-gather.11
  244.6 40.2 reduce-scatter.12
  287.8 42.7 all-gather.13
  357.0 40.2 reduce-scatter.14
  400.7 42.7 all-gather.15
  445.7 42.3 all-gather.17
  506.6 40.2 reduce-scatter.18
  549.8 40.6 reduce-scatter.16
  597.5 42.7 all-gather.19
  674.1 40.2 reduce-scatter.20
  716.4 42.7 all-gather.21
  761.2 42.3 all-gather.23
  821.1 40.2 reduce-scatter.24
  864.2 40.6 reduce-scatter.28
  908.1 42.7 all-gather.25
  989.8 40.2 reduce-scatter.26
  1036.4 192.6 all-reduce.4
where the time goes:
time: 1260 us; the launch traced here: 1250 us
  waiting for transfers between devices  847 us (67%)
  matrix products  176 us (14%)
  other arithmetic  71.9 us (6%)
  local copies, waits for them, and re-layouts  68.4 us (5%)
  blocking collectives  65.3 us (5%)
  between operations  16.3 us (1%)
    reduce_scatter x6, waiting for transfers between devices, branch_rows(): lax.psum_scatter(matmul(source, weight).astype(jnp.bfloat16), 'mp', scatt...  232 us
    all_gather x5, waiting for transfers between devices, gather_rows(): return lax.all_gather(source, 'mp', axis=0, tiled=True)  207 us
    all_gather x4, waiting for transfers between devices, gather_grads(): return lax.all_gather(source, 'mp', axis=0, tiled=True)  163 us
    psum x1, waiting for transfers between devices, body(): lax.psum((teacher_large[0], teacher_large[1], teacher_large[2], teacher_l...  139 us
    reduce_scatter x4, waiting for transfers between devices, input_rows(): lax.psum_scatter(summed.astype(jnp.bfloat16), 'mp', scatter_dimension=0,...  103 us
    dot_general x14, matrix products, matmul(): return jnp.dot(left_side, right_side, preferred_element_type=jnp.float32)  53.3 us
    dot_general x12, matrix products, matmul_nt(): lax.dot_general(left_side, right_side, (((1,), (1,)), ((), ())), preferre...  46.3 us
    psum x1, blocking collectives, body(): lax.psum((teacher_small[0], teacher_small[1], teacher_small[2], teacher_s...  40.8 us
  transfers between devices with their start and end apart: 20, of which 19 were waited for; matrix products, arithmetic and copies ran while one was open for 7% of the time, Pallas kernels for 0%

commit v1 on v0

v1 whole, which is shorter than its diff:
```python
import functools

import jax
import jax.numpy as jnp
from jax import lax
from jax.experimental import pallas as pl
from jax.experimental.pallas import tpu as pltpu
from jax.sharding import PartitionSpec as P

HEAD_DIM = 64
SLOT = 640
PARTS = 8
BF = jnp.bfloat16
F32 = jnp.float32

epsilon = 1e-06


def layer_norm(values, norm_gain, norm_shift):
    center = values - jnp.mean(values, axis=-1, keepdims=True)
    spread = jnp.mean(center * center, axis=-1, keepdims=True)
    inverse = lax.rsqrt(spread + epsilon)
    unit = center * inverse
    return unit * norm_gain + norm_shift, unit, inverse


def layer_norm_back(grad, unit, inverse, norm_gain):
    scaled = grad * norm_gain
    return (
        inverse
        * (
            scaled
            - jnp.mean(scaled, axis=-1, keepdims=True)
            - unit * jnp.mean(scaled * unit, axis=-1, keepdims=True)
        ),
        jnp.sum(grad * unit, axis=0),
        jnp.sum(grad, axis=0),
    )


def gelu_exact(values):
    return jax.nn.gelu(values, approximate=False)


def matmul(left_side, right_side):
    return jnp.dot(left_side, right_side, preferred_element_type=F32)


def matmul_tn(left_side, right_side):
    return lax.dot_general(
        left_side, right_side, (((0,), (0,)), ((), ())), preferred_element_type=F32
    )


def matmul_nt(left_side, right_side):
    return lax.dot_general(
        left_side, right_side, (((1,), (1,)), ((), ())), preferred_element_type=F32
    )


def swap(source, axis, bit):
    count = lax.axis_size(axis)
    return lax.ppermute(source, axis, [(i, i ^ bit) for i in range(count)])


def low_index():
    return lax.rem(lax.axis_index("dp"), PARTS)


MESH = pl.DeviceIdType.MESH
ORDERS = ((2, 4), (4, 2), (2, 4), (4, 2), (2, 4), (4, 2))
COUNT = len(ORDERS)
AHEAD = 2


def flip(index, bits):
    bit = 1
    while bit <= bits:
        if bits & bit:
            index = index + bit - 2 * bit * lax.rem(lax.div(index, bit), 2)
        bit *= 2
    return index


def partners(dp_size):
    bits = []
    bit = 1
    while bit < dp_size:
        bits.append({"dp": bit})
        bit *= 2
    return bits + [{"mp": r} for r in (1, 2, 3)]


def device_at(bits):
    return {axis: flip(lax.axis_index(axis), bit) for axis, bit in bits.items()}


def enter(dp_size):
    barrier = pltpu.get_barrier_semaphore()
    for bits in partners(dp_size):
        pl.semaphore_signal(barrier, inc=1, device_id=device_at(bits), device_id_type=MESH)
    pl.semaphore_wait(barrier, len(partners(dp_size)))


def remote(source, target, send, recv, bits):
    return pltpu.make_async_remote_copy(
        src_ref=source,
        dst_ref=target,
        send_sem=send,
        recv_sem=recv,
        device_id=device_at(bits),
        device_id_type=MESH,
    )


def piece_rows(index, size):
    return pl.ds(pl.multiple_of(index * size, size), size)


def gather_kernel(dp_size, *refs):
    local = refs[:COUNT]
    full = refs[COUNT : 2 * COUNT]
    send, recv = refs[2 * COUNT :]
    size = local[0].shape[0] // PARTS
    me = lax.rem(lax.axis_index("dp"), PARTS)
    enter(dp_size)

    def rows(mask):
        return piece_rows(flip(me, mask), size)

    def slab(i, mask):
        return full[i].at[:, rows(mask)]

    def along_z(i):
        return [
            remote(
                local[i].at[rows(0)],
                full[i].at[r - 1, rows(0)],
                send.at[i, r - 1],
                recv.at[i, r - 1],
                {"mp": r},
            )
            for r in (1, 2, 3)
        ]

    def along_dp(i, slot, mask, bit):
        return remote(
            slab(i, mask), slab(i, mask), send.at[i, slot], recv.at[i, slot], {"dp": bit}
        )

    flying = []

    def launch(copies):
        for copy in copies:
            copy.start()
        flying.extend(copies)
        return copies

    def landed(copies):
        for copy in copies:
            copy.wait_recv()

    state = [None] * COUNT

    def stage(i, s):
        first, second = ORDERS[i]
        if s == 0:
            landed(state[i])
            if i + AHEAD < COUNT:
                state[i + AHEAD] = launch(along_z(i + AHEAD))
            state[i] = launch([along_dp(i, 3, 0, first), along_dp(i, 4, 0, second)])
        elif s == 1:
            landed(state[i][:1])
            state[i] = [state[i][1]] + launch([along_dp(i, 5, first, second)])
            launch([along_dp(i, 6, 0, 1), along_dp(i, 7, first, 1)])
        elif s == 2:
            landed(state[i])
            launch([along_dp(i, 8, second, 1), along_dp(i, 9, first | second, 1)])

    for i in range(AHEAD):
        state[i] = launch(along_z(i))
    for t in range(COUNT + 2):
        for s in (0, 1, 2):
            if 0 <= t - s < COUNT:
                stage(t - s, s)
    for i in range(COUNT):
        for slot, mask in ((6, 0), (7, ORDERS[i][0]), (8, ORDERS[i][1]), (9, 6)):
            along_dp(i, slot, mask, 1).wait_recv()
    for copy in flying:
        copy.wait_send()


def gather_all(locals_):
    dp_size = lax.axis_size("dp")
    anywhere = pl.BlockSpec(memory_space=pl.ANY)
    got = pl.pallas_call(
        functools.partial(gather_kernel, dp_size),
        out_shape=[jax.ShapeDtypeStruct((3,) + local.shape, BF) for local in locals_],
        in_specs=[anywhere] * COUNT,
        out_specs=[anywhere] * COUNT,
        scratch_shapes=[
            pltpu.SemaphoreType.DMA((COUNT, 10)),
            pltpu.SemaphoreType.DMA((COUNT, 10)),
        ],
        compiler_params=pltpu.CompilerParams(collective_id=0, has_side_effects=True),
    )(*locals_)
    return [jnp.concatenate([local[None], rest]) for local, rest in zip(locals_, got)]


def reduce_kernel(dp_size, *refs):
    grad = refs[:COUNT]
    out = refs[COUNT : 2 * COUNT]
    (core_in, own, first_in, second_in, more_in, z_in, whole, wide, send, recv, load, store) = (
        refs[2 * COUNT :]
    )
    size = out[0].shape[0] // PARTS
    me = lax.rem(lax.axis_index("dp"), PARTS)
    more = []
    bit = PARTS
    while bit < dp_size:
        more.append(bit)
        bit *= 2

    def rows(mask):
        return piece_rows(flip(me, mask), size)

    def masks(i):
        first, second = ORDERS[i]
        return (0, second, first, first | second)

    flying = []

    def launch(copies):
        for copy in copies:
            copy.start()
        flying.extend(copies)
        return copies

    def landed(copies):
        for copy in copies:
            copy.wait_recv()

    def loads(i):
        return [
            pltpu.make_async_copy(grad[i].at[:, rows(mask)], own.at[i % 2, k], load.at[i % 2, k])
            for k, mask in enumerate(masks(i))
        ]

    def added(left, right):
        left[...] = (left[...].astype(F32) + right[...].astype(F32)).astype(BF)

    def add_slabs(target, source):
        @pl.loop(0, 4)
        def _(r):
            added(target.at[r], source.at[r])

    def across(i):
        return [
            remote(
                grad[i].at[:, rows(1 | mask)],
                core_in.at[i, k],
                send.at[i, k],
                recv.at[i, k],
                {"dp": 1},
            )
            for k, mask in enumerate(masks(i))
        ]

    state = [None] * COUNT

    def stage(i, s):
        first, second = ORDERS[i]
        if s == 0:
            landed(state[i])
            if i + AHEAD < COUNT:
                state[i + AHEAD] = launch(across(i + AHEAD))
            for copy in loads(i):
                copy.wait()
            for k in (2, 3):
                add_slabs(core_in.at[i, k], own.at[i % 2, k])
            state[i] = launch(
                [
                    remote(
                        core_in.at[i, pl.ds(2, 2)],
                        first_in.at[i],
                        send.at[i, 4],
                        recv.at[i, 4],
                        {"dp": first},
                    )
                ]
            )
            for k in (0, 1):
                add_slabs(core_in.at[i, k], own.at[i % 2, k])
            if i + 2 < COUNT:
                for copy in loads(i + 2):
                    copy.start()
        elif s == 1:
            landed(state[i])
            add_slabs(core_in.at[i, 1], first_in.at[i, 1])
            state[i] = launch(
                [
                    remote(
                        core_in.at[i, 1],
                        second_in.at[i],
                        send.at[i, 5],
                        recv.at[i, 5],
                        {"dp": second},
                    )
                ]
            )
            add_slabs(core_in.at[i, 0], first_in.at[i, 0])
        elif s == 2:
            landed(state[i])
            add_slabs(core_in.at[i, 0], second_in.at[i])
            for e, bit in enumerate(more):
                copy = remote(
                    core_in.at[i, 0],
                    more_in.at[i, e],
                    send.at[i, 16 + e],
                    recv.at[i, 16 + e],
                    {"dp": bit},
                )
                copy.start()
                copy.wait()
                add_slabs(core_in.at[i, 0], more_in.at[i, e])
            state[i] = launch(
                [
                    remote(
                        core_in.at[i, 0, r],
                        z_in.at[i, r - 1],
                        send.at[i, 5 + r],
                        recv.at[i, 5 + r],
                        {"mp": r},
                    )
                    for r in (1, 2, 3)
                ]
            )
        elif s == 3:
            landed(state[i])
            total = core_in[i, 0, 0].astype(F32)
            for r in range(3):
                total = total + z_in[i, r].astype(F32)
            whole[i, rows(0), :] = total.astype(BF)
            state[i] = launch([spread(i, 9, 0, first), spread(i, 10, 0, second)])
        elif s == 4:
            landed(state[i][:1])
            state[i] = [state[i][1]] + launch([spread(i, 11, first, second)])
            launch([spread(i, 12, 0, 1), spread(i, 13, first, 1)])
        elif s == 5:
            landed(state[i])
            launch([spread(i, 14, second, 1), spread(i, 15, first | second, 1)])
            state[i] = [
                spread(i, 12, 0, 1),
                spread(i, 13, first, 1),
                spread(i, 14, second, 1),
                spread(i, 15, first | second, 1),
            ]
        elif s == 6:
            landed(state[i])
            if i >= 2:
                pltpu.make_async_copy(wide.at[i % 2], out[i - 2], store.at[i % 2]).wait()
            wide_i = wide.at[i % 2]

            @pl.loop(0, PARTS)
            def _(p):
                part = piece_rows(p, size)
                wide_i[part, :] = whole[i, part, :].astype(F32)

            pltpu.make_async_copy(wide.at[i % 2], out[i], store.at[i % 2]).start()

    def spread(i, slot, mask, bit):
        place = whole.at[i, rows(mask)]
        return remote(place, place, send.at[i, slot], recv.at[i, slot], {"dp": bit})

    for i in (0, 1):
        for copy in loads(i):
            copy.start()
    enter(dp_size)
    for i in range(AHEAD):
        state[i] = launch(across(i))
    for t in range(COUNT + 6):
        for s in range(7):
            if 0 <= t - s < COUNT:
                stage(t - s, s)
    for i in (COUNT - 2, COUNT - 1):
        pltpu.make_async_copy(wide.at[i % 2], out[i], store.at[i % 2]).wait()
    for copy in flying:
        copy.wait_send()


def reduce_all(grads):
    dp_size = lax.axis_size("dp")
    anywhere = pl.BlockSpec(memory_space=pl.ANY)
    rows, columns = grads[0].shape[1:]
    size = rows // PARTS
    more = max(1, (dp_size // PARTS).bit_length() - 1)
    return pl.pallas_call(
        functools.partial(reduce_kernel, dp_size),
        out_shape=[jax.ShapeDtypeStruct((rows, columns), F32)] * COUNT,
        in_specs=[anywhere] * COUNT,
        out_specs=[anywhere] * COUNT,
        scratch_shapes=[
            pltpu.VMEM((COUNT, 4, 4, size, columns), BF),
            pltpu.VMEM((2, 4, 4, size, columns), BF),
            pltpu.VMEM((COUNT, 2, 4, size, columns), BF),
            pltpu.VMEM((COUNT, 4, size, columns), BF),
            pltpu.VMEM((COUNT, more, 4, size, columns) if dp_size > PARTS else (1, 1, 4, 16, 128), BF),
            pltpu.VMEM((COUNT, 3, size, columns), BF),
            pltpu.VMEM((COUNT, rows, columns), BF),
            pltpu.VMEM((2, rows, columns), F32),
            pltpu.SemaphoreType.DMA((COUNT, 16 + more)),
            pltpu.SemaphoreType.DMA((COUNT, 16 + more)),
            pltpu.SemaphoreType.DMA((2, 4)),
            pltpu.SemaphoreType.DMA((2,)),
        ],
        compiler_params=pltpu.CompilerParams(
            collective_id=1, has_side_effects=True, vmem_limit_bytes=60 * 1024 * 1024
        ),
    )(*grads)


def reduce_rows(rows):
    for axis in ("mp", "dp"):
        bit = 1
        while bit < lax.axis_size(axis):
            rows = rows + swap(rows, axis, bit)
            bit *= 2
    return rows


def relative(chunks):
    return jnp.take(chunks, jnp.arange(4) ^ lax.axis_index("mp"), axis=0)


def heads_of(values):
    return values.reshape(values.shape[0], -1, HEAD_DIM)


def forward_block(resid, key_valid, small, full):
    gains, shifts, in_bias, out_bias, scales, up_bias = small
    attn_w, up_w, down_w = full
    normed, unit0, inverse0 = layer_norm(resid, gains[0], shifts[0])
    normed = normed.astype(BF)
    normed_all = jnp.concatenate([normed, swap(normed, "mp", 1)])
    wq = attn_w[:, 0:192].reshape(768, 768)
    wk = attn_w[:, 192:384].reshape(768, 768)
    wv = attn_w[:, 384:576].reshape(768, 768)
    wo = attn_w[:, 576:768].reshape(768, 768)
    query = (matmul_nt(normed, wq) + in_bias[0]).astype(BF)
    key = matmul_nt(normed_all, wk).astype(BF)
    value = (matmul_nt(normed_all, wv) + in_bias[1]).astype(BF)
    scores = jnp.einsum(
        "qhd,khd->hqk", heads_of(query), heads_of(key), preferred_element_type=F32
    ) * HEAD_DIM ** (-0.5)
    scores = jnp.where(key_valid[None, None, :], scores, -1e30)
    peak = jnp.max(scores, axis=-1, keepdims=True)
    exponent = jnp.exp(scores - peak)
    total = jnp.sum(exponent, axis=-1, keepdims=True)
    probs = (exponent / total).astype(BF)
    mixed = jnp.einsum("hqk,khd->qhd", probs, heads_of(value), preferred_element_type=F32)
    mixed = mixed.reshape(query.shape).astype(BF)
    log_total = peak + jnp.log(total)
    attn = matmul(mixed, wo) + out_bias[0]
    middle = resid + scales[0] * attn
    normed2, unit1, inverse1 = layer_norm(middle, gains[1], shifts[1])
    normed2 = normed2.astype(BF)
    pre = jnp.stack([matmul(normed2, up_w[r]) + up_bias[r] for r in range(4)], axis=1)
    hidden = gelu_exact(pre).astype(BF)
    mlp = (
        matmul(hidden.reshape(hidden.shape[0], -1), down_w.reshape(-1, 768)) + out_bias[1]
    )
    result = middle + scales[1] * mlp
    kept = (
        unit0,
        inverse0,
        normed_all,
        query,
        key,
        value,
        log_total,
        mixed,
        attn,
        unit1,
        inverse1,
        normed2,
        pre,
        hidden,
        mlp,
    )
    return result, kept


def backward_block(grad, key_valid, small, full, kept):
    gains, shifts, in_bias, out_bias, scales, up_bias = small
    attn_w, up_w, down_w = full
    (
        unit0,
        inverse0,
        normed_all,
        query,
        key,
        value,
        log_total,
        mixed,
        attn,
        unit1,
        inverse1,
        normed2,
        pre,
        hidden,
        mlp,
    ) = kept
    rows = grad.shape[0]
    scale_mlp = jnp.sum(grad * mlp, axis=0)
    grad_branch = (scales[1] * grad).astype(BF)
    bias_mlp = jnp.sum(grad_branch.astype(F32), axis=0)
    grad_down = jnp.stack([matmul_tn(hidden[:, r], grad_branch).astype(BF) for r in range(4)])
    grad_hidden = matmul_nt(grad_branch, down_w.reshape(-1, 768)).reshape(pre.shape)
    value_, gelu_back = jax.vjp(gelu_exact, pre)
    grad_pre = gelu_back(grad_hidden)[0].astype(BF)
    grad_up_bias = jnp.sum(grad_pre.astype(F32), axis=0)
    grad_up = jnp.stack([matmul_tn(normed2, grad_pre[:, r]).astype(BF) for r in range(4)])
    grad_normed2 = sum(matmul_nt(grad_pre[:, r], up_w[r]) for r in range(4))
    grad_middle, gain_mlp, shift_mlp = layer_norm_back(grad_normed2, unit1, inverse1, gains[1])
    grad_middle = grad + grad_middle
    scale_attn = jnp.sum(grad_middle * attn, axis=0)
    grad_attn = (scales[0] * grad_middle).astype(BF)
    bias_attn = jnp.sum(grad_attn.astype(F32), axis=0)
    wq = attn_w[:, 0:192].reshape(768, 768)
    wk = attn_w[:, 192:384].reshape(768, 768)
    wv = attn_w[:, 384:576].reshape(768, 768)
    wo = attn_w[:, 576:768].reshape(768, 768)
    grad_wo = matmul_tn(mixed, grad_attn).astype(BF)
    grad_mixed = matmul_nt(grad_attn, wo).astype(BF)
    scores = jnp.einsum(
        "qhd,khd->hqk", heads_of(query), heads_of(key), preferred_element_type=F32
    ) * HEAD_DIM ** (-0.5)
    scores = jnp.where(key_valid[None, None, :], scores, -1e30)
    probs = jnp.exp(scores - log_total)
    grad_probs = jnp.einsum(
        "qhd,khd->hqk", heads_of(grad_mixed), heads_of(value), preferred_element_type=F32
    )
    grad_value = jnp.einsum(
        "hqk,qhd->khd", probs.astype(BF), heads_of(grad_mixed), preferred_element_type=F32
    )
    inner = jnp.sum(probs * grad_probs, axis=-1, keepdims=True)
    grad_scores = (probs * (grad_probs - inner)).astype(BF)
    grad_query = jnp.einsum(
        "hqk,khd->qhd", grad_scores, heads_of(key), preferred_element_type=F32
    )
    grad_key = jnp.einsum(
        "hqk,qhd->khd", grad_scores, heads_of(query), preferred_element_type=F32
    )
    scale = HEAD_DIM ** (-0.5)
    grad_query = (grad_query * scale).astype(BF).reshape(query.shape)
    grad_key = (grad_key * scale).astype(BF).reshape(key.shape)
    grad_value = grad_value.astype(BF).reshape(key.shape)
    grad_in = [
        matmul_tn(grad_query, normed_all[:rows]).astype(BF).reshape(4, 192, 768),
        matmul_tn(grad_key, normed_all).astype(BF).reshape(4, 192, 768),
        matmul_tn(grad_value, normed_all).astype(BF).reshape(4, 192, 768),
        grad_wo.reshape(4, 192, 768),
    ]
    grad_attn_w = jnp.concatenate(grad_in, axis=1)
    grad_in_bias = jnp.stack(
        [
            jnp.sum(grad_query.astype(F32), axis=0),
            jnp.sum(grad_value.astype(F32), axis=0),
        ]
    )
    away = matmul(grad_key[rows:], wk) + matmul(grad_value[rows:], wv)
    grad_normed = (
        matmul(grad_query, wq)
        + matmul(grad_key[:rows], wk)
        + matmul(grad_value[:rows], wv)
        + swap(away.astype(BF), "mp", 1).astype(F32)
    )
    grad_resid, gain_attn, shift_attn = layer_norm_back(grad_normed, unit0, inverse0, gains[0])
    grad_resid = grad_middle + grad_resid
    packed = jnp.stack(
        [
            gain_attn,
            gain_mlp,
            shift_attn,
            shift_mlp,
            bias_attn,
            bias_mlp,
            scale_attn,
            scale_mlp,
        ]
    )
    in_bias_abs = relative(grad_in_bias.reshape(2, 4, 192).swapaxes(0, 1))
    packed = jnp.concatenate(
        [packed, in_bias_abs.reshape(2, 768), relative(grad_up_bias).reshape(4, 768)]
    )
    packed = reduce_rows(packed)
    in_bias_abs = packed[8:10].reshape(4, 2, 192)
    mine = lax.axis_index("mp")
    in_bias_out = lax.dynamic_index_in_dim(in_bias_abs, mine, 0, keepdims=False)
    up_bias_out = lax.dynamic_index_in_dim(packed[10:14], mine, 0, keepdims=False)
    rest = (packed, in_bias_out, up_bias_out)
    return grad_resid, (grad_down, grad_up, grad_attn_w), rest


def arrange(reduced, rest):
    grad_down, grad_up, grad_attn_w = reduced
    packed, in_bias_out, up_bias_out = rest
    return (
        packed[0:2],
        packed[2:4],
        grad_attn_w[:576].reshape(3, 192, 768).swapaxes(1, 2),
        in_bias_out,
        grad_attn_w[576:],
        packed[4:6],
        packed[6:8],
        grad_up,
        up_bias_out,
        grad_down,
    )


def local_block(weights):
    gains, shifts, p_in, p_bias, p_out, out_bias, scales, up, up_bias, down = weights
    attn_local = jnp.concatenate([p_in.swapaxes(1, 2).reshape(-1, p_in.shape[1]), p_out])
    return [attn_local, up, down]


def gather_small(project_bias, up_bias):
    bias = lax.all_gather(
        jnp.concatenate([project_bias.reshape(-1), up_bias]), "mp", axis=0, tiled=False
    )
    bias = relative(bias)
    in_bias = bias[:, :384].reshape(4, 2, 192).swapaxes(0, 1).reshape(2, 768)
    return in_bias, bias[:, 384:]


def body(inputs, lengths, cotangent, *params):
    student, teacher = params[:10], params[10:]
    z = lax.axis_index("mp")
    length = lax.dynamic_index_in_dim(lengths, z // 2, 0, keepdims=False)
    rows = inputs.shape[0]
    half = lax.rem(z, 2)
    position = jnp.concatenate(
        [half * rows + jnp.arange(rows), (1 - half) * rows + jnp.arange(rows)]
    )
    key_valid = position < length

    def prepare(weights):
        gains, shifts, p_in, p_bias, p_out, out_bias, scales, up, up_bias, down = weights
        in_bias, up_bias_all = gather_small(p_bias, up_bias)
        return (gains, shifts, in_bias, out_bias, scales, up_bias_all)

    full = gather_all(local_block(student) + local_block(teacher))
    student_full, teacher_full = full[:3], full[3:]
    student_small = prepare(student)
    teacher_small = prepare(teacher)
    start_rows = inputs.astype(F32)
    student_out, student_kept = forward_block(start_rows, key_valid, student_small, student_full)
    teacher_out, teacher_kept = forward_block(student_out, key_valid, teacher_small, teacher_full)
    grad_mid, teacher_large, teacher_rest = backward_block(
        cotangent.astype(F32), key_valid, teacher_small, teacher_full, teacher_kept
    )
    grad_input, student_large, student_rest = backward_block(
        grad_mid, key_valid, student_small, student_full, student_kept
    )
    reduced = reduce_all(teacher_large + student_large)
    return (
        (teacher_out.astype(BF), grad_input.astype(BF))
        + arrange(reduced[3:], student_rest)
        + arrange(reduced[:3], teacher_rest)
    )


def solution(mesh):
    rows = P(("dp", "mp"), None)
    weights = (
        P(),
        P(),
        P(None, None, "mp"),
        P(None, "mp"),
        P("mp", None),
        P(),
        P(),
        P(None, "mp"),
        P("mp"),
        P("mp", None),
    )
    in_specs = (rows, P("dp"), rows) + weights + weights
    out_specs = (rows, rows) + weights + weights
    return jax.shard_map(body, mesh=mesh, in_specs=in_specs, out_specs=out_specs, check_vma=False)
```

time: 1260 us -> 656 us (0.52)
  waiting for transfers between devices: 847 us -> 22.1 us
  Pallas kernels: 0 us -> 288 us
  blocking collectives: 65.3 us -> 32.2 us
  matrix products: 176 us -> 147 us
  starting transfers between devices: 2.62 us -> 27.6 us
  between operations: 16.3 us -> 3.04 us
    all_gather x9 -> x0, waiting for transfers between devices: 371 us -> none  [the longest x5 207 us: gather_rows(): return lax.all_gather(source, 'mp', axis=0, tiled=True)]
    reduce_scatter x10 -> x0, waiting for transfers between devices: 336 us -> none  [the longest x6 232 us: branch_rows(): lax.psum_scatter(matmul(source, weight).astype(jnp.bfloat16), 'mp', scatt...]
    pallas_call x0 -> x2, Pallas kernels: none -> 288 us  [the longest x1 175 us: reduce_all(): pl.pallas_call(functools.partial(reduce_kernel, dp_size), out_shape=[jax....]
    psum x1 -> x0, waiting for transfers between devices: 139 us -> none  [body(): lax.psum((teacher_large[0], teacher_large[1], teacher_large[2], teacher_l...]
    psum x2 -> x0, blocking collectives: 65.3 us -> none  [the longest x1 40.8 us: body(): lax.psum((teacher_small[0], teacher_small[1], teacher_small[2], teacher_s...]
    all_gather x0 -> x2, blocking collectives: none -> 32.2 us  [gather_small(): lax.all_gather(jnp.concatenate([project_bias.reshape(-1), up_bias]), 'mp'...]
    dot_general x44 -> x34, matrix products: 98.9 us -> 67.8 us  [the longest x22 29.4 us: matmul(): return jnp.dot(left_side, right_side, preferred_element_type=F32)]
    dot_general x12 -> x24, matrix products: 21.1 us -> 49.5 us  [matmul_tn(): lax.dot_general(left_side, right_side, (((0,), (0,)), ((), ())), preferre...]
  transfers between devices with their start and end apart: 20 -> 14, of which waited for: 19 -> 7; matrix products, arithmetic and copies ran while one was open for 7% -> 13% of each run, Pallas kernels for 0% -> 44%
where the time goes in v1:
time: 656 us; the launch traced here: 652 us
  Pallas kernels  288 us (44%)
  matrix products  147 us (22%)
  other arithmetic  75.2 us (11%)
  local copies, waits for them, and re-layouts  57.4 us (9%)
  blocking collectives  32.2 us (5%)
  starting transfers between devices  27.6 us (4%)
  waiting for transfers between devices  22.1 us (3%)
    pallas_call x1, Pallas kernels, reduce_all(): pl.pallas_call(functools.partial(reduce_kernel, dp_size), out_shape=[jax....  175 us
    pallas_call x1, Pallas kernels, gather_all(): pl.pallas_call(functools.partial(gather_kernel, dp_size), out_shape=[jax....  113 us
    dot_general x24, matrix products, matmul_tn(): lax.dot_general(left_side, right_side, (((0,), (0,)), ((), ())), preferre...  49.5 us
    all_gather x2, blocking collectives, gather_small(): lax.all_gather(jnp.concatenate([project_bias.reshape(-1), up_bias]), 'mp'...  32.2 us
    dot_general x22, matrix products, matmul(): return jnp.dot(left_side, right_side, preferred_element_type=F32)  29.4 us
    dot_general x18, matrix products, matmul_nt(): lax.dot_general(left_side, right_side, (((1,), (1,)), ((), ())), preferre...  29.3 us
    ppermute x14, starting transfers between devices, swap(): return lax.ppermute(source, axis, [(i, i ^ bit) for i in range(count)])  27.6 us
    ppermute x14, waiting for transfers between devices, swap(): return lax.ppermute(source, axis, [(i, i ^ bit) for i in range(count)])  22.1 us
  transfers between devices with their start and end apart: 14, of which 7 were waited for; matrix products, arithmetic and copies ran while one was open for 13% of the time, Pallas kernels for 44%

profile of v1, /device:TPU:0, one launch (start us, length us, event | category | flops | bytes accessed | tf_op | source)
XLA Modules:
  0.0 651.9 jit_solution(2329154811524065615)
XLA Ops:
  5.4 3.1 collective-permute-start
  10.0 19.1 %all-gather.3 = f32[4,1,1152]{2,1,0:T(1,128)S(1)} all-gather(f32[1,1,1152]{2,1,0:T(1,128)S(1)} %reshape.474), channel_id=3, replica_groups=mesh['dp'=8,'mp'=4] {'mp'}, dimensions={0}, use_global_device_ids=true | all-gather | bytes 23040 | tf_op jit(solution)/shard_map/all_gather | solution.py:629
  30.6 13.1 %all-gather.2 = f32[4,1,1152]{2,1,0:T(1,128)S(1)} all-gather(f32[1,1,1152]{2,1,0:T(1,128)S(1)} %reshape.472), channel_id=2, replica_groups=mesh['dp'=8,'mp'=4] {'mp'}, dimensions={0}, use_global_device_ids=true | all-gather | bytes 23040 | tf_op jit(solution)/shard_map/all_gather | solution.py:629
  45.3 2.8 fusion.143
  50.3 112.9 %shard_map.390 = (bf16[3,768,768]{2,1,0:T(8,128)(2,1)}, bf16[3,768,768]{2,1,0:T(8,128)(2,1)}, bf16[3,768,768]{2,1,0:T(8,128)(2,1)}, bf16[3,768,768]{2,1,0:T(8,12...) custom-call(bf16[768,768]{1,0:T(8,128)(2,1)} %get-tuple-element.128.refs_0_, ...), custom_call_target="tpu_custom_call" | custom-call | tf_op jit(solution)/shard_map/pallas_call | solution.py:196
  163.2 6.3 pad_maximum_fusion.26
  179.0 2.9 add_convert_fusion.3
  188.6 2.6 fusion
  192.4 3.3 fusion.63
  200.7 9.5 %multiply_convert_fusion.3 = (bf16[320,4,768]{2,0,1:T(8,128)(2,1)S(1)}, f32[320,4,768]{2,0,1:T(8,128)}) fusion(f32[320,1,768]{2,0,1:T(8,128)S(1)} %fusion.58, f32[320,1,768]{2,0,1:T(8,128)S(1)} %fusion.59, f32[320,1,768]{2,0,1:T(8,128)S(1)} %fusion.60, f32[320,1,768]{2,0,1:T(8,128)S(1)} %fusion.61), kind=kLoop, calls=%fused_computation.73 | loop fusion | flops 66846720 | bytes 9830400 | tf_op jit(solution)/shard_map/convert_element_type | solution.py:468
  210.3 2.7 fusion.146
  214.3 8.4 %collective-permute-start.1 = (bf16[320,768]{1,0:T(8,128)(2,1)}, bf16[320,768]{1,0:T(8,128)(2,1)}, u32[]{:S(2)}, u32[]{:S(2)}) collective-permute-start(bf16[320,768]{1,0:T(8,128)(2,1)} %add_convert_fusion.6), channel_id=1, source_target_pairs={{0,1},{1,0},{2,3},{3,2},{4,5},{5,4},{6,7},{7,6},{8,9},{9,8},{10,11... | collective-permute-start | bytes 1474568 | tf_op jit(solution)/shard_map/ppermute | solution.py:63
  225.5 9.4 %collective-permute-done.1 = bf16[320,768]{1,0:T(8,128)(2,1)} collective-permute-done((bf16[320,768]{1,0:T(8,128)(2,1)}, bf16[320,768]{1,0:T(8,128)(2,1)}, u32[]{:S(2)}, u32[]{:S(2)}) %collective-permute-start.1) | collective-permute-done | bytes 491552 | tf_op jit(solution)/shard_map/ppermute | solution.py:63
  234.9 3.5 add_convert_fusion.2
  240.7 3.1 convolution_convert_fusion.24
  245.3 3.2 fusion.13
  248.5 2.6 fusion.1
  252.3 3.3 fusion.62
  260.2 8.5 %multiply_convert_fusion.2 = (bf16[320,4,768]{2,0,1:T(8,128)(2,1)S(1)}, f32[320,4,768]{2,0,1:T(8,128)S(1)}) fusion(f32[320,1,768]{2,0,1:T(8,128)S(1)} %fusion.54, f32[320,1,768]{2,0,1:T(8,128)S(1)} %fusion.55, f32[320,1,768]{2,0,1:T(8,128)S(1)} %fusion.56, f32[320,1,768]{2,0,1:T(8,128)S(1)} %fusion.57), kind=kLoop, calls=%fused_computation.60 | loop fusion | flops 66846720 | bytes 9830400 | tf_op jit(solution)/shard_map/convert_element_type | solution.py:468
  268.7 3.5 convert_reduce_fusion
  275.0 3.4 fusion.118
  283.6 8.1 %multiply_reduce_fusion.1 = (f32[12,320]{1,0:T(8,128)S(1)}, f32[12,320,640]{2,1,0:T(8,128)S(1)}) fusion(f32[12,320]{1,0:T(8,128)S(1)} %log_add_fusion.1, f32[12,320,640]{2,1,0:T(8,128)} %copy-done.1, pred[640]{0:T(1024)(128)(4,1)S(1)} %add_compare_fusion, bf16[320,12,64]{0,2,1:T(8,128)(2,1)} %bitcast.397, bf16[640,12,64]{0,2,1:T(8,128)(2,1)} %bitcast.395), kind=kOutput, calls=%fused_computation.10 | convolution fusion | flops 326856960 | bytes 21166720 | tf_op jit(solution)/shard_map/qhd,khd->hqk/dot_general | solution.py:540
  291.7 2.9 convert_reduce_fusion.2
  294.6 3.2 multiply_convert_fusion.1
  318.9 2.8 convolution_convert_fusion.11
  327.9 3.1 convolution_add_fusion.8
  331.0 3.7 pad_maximum_fusion.2.refs_0_
  334.8 2.6 pad_maximum_fusion.3.refs_1_
  337.3 3.4 convolution_convert_fusion.22
  340.7 3.4 convolution_convert_fusion.23
  345.4 6.1 pad_maximum_fusion.4.refs_2_
  351.6 2.8 multiply_reduce_fusion.4
  357.4 3.2 convert_reduce_fusion.1
  368.3 7.4 %multiply_reduce_fusion = (f32[12,320]{1,0:T(8,128)S(1)}, f32[12,320,640]{2,1,0:T(8,128)S(1)}) fusion(f32[12,320]{1,0:T(8,128)S(1)} %log_add_fusion, f32[12,320,640]{2,1,0:T(8,128)} %copy-done, pred[640]{0:T(1024)(128)(4,1)S(1)} %add_compare_fusion, bf16[320,12,64]{0,2,1:T(8,128)(2,1)} %bitcast.399, bf16[640,12,64]{0,2,1:T(8,128)(2,1)S(1)} %bitcast.394), kind=kOutput, calls=%fused_computation.7 | convolution fusion | flops 326856960 | bytes 21166720 | tf_op jit(solution)/shard_map/qhd,khd->hqk/dot_general | solution.py:540
  375.8 2.9 convert_reduce_fusion.3
  378.7 3.0 multiply_convert_fusion
  406.3 2.8 convolution_convert_fusion.1
  411.3 4.0 pad_maximum_fusion.5.refs_3_
  415.4 2.7 pad_maximum_fusion.6.refs_4_
  423.3 2.6 collective-permute-done.10
  429.6 3.0 collective-permute-done.12
  435.7 174.9 %shard_map.391 = (f32[768,768]{1,0:T(8,128)}, f32[768,768]{1,0:T(8,128)}, f32[768,768]{1,0:T(8,128)}, f32[768,768]{1,0:T(8,128)}, f32[768,768]{1,0:T(8,128)}, /*index=5*/f32[768,768]{1,0:T(8,128)}) custom-call(bf16[4,768,768]{2,1,0:T(8,128)(2,1)} %pad_maximum_fusion.2.refs_0_, bf16[4,768,768]{2,1,0:T(8,128)(2,1)} %pad_maximum_fusion.3.refs_1_, ...), custom_call_target="tpu_custom_call" | custom-call | tf_op jit(solution)/shard_map/pallas_call | solution.py:397
  610.6 2.9 slice.398
  618.1 3.1 fusion.115
  621.3 3.6 collective-permute-start.4
  635.2 2.6 collective-permute-done.7
  639.6 2.5 fusion.114
  644.0 3.4 copy.87
  (502 shorter events, 154.9 us)
Async XLA Ops:
  0.7 47.5 %copy-start.108 = (bf16[192,768]{1,0:T(8,128)(2,1)S(1)}, bf16[192,768]{1,0:T(8,128)(2,1)}, u32[]{:S(2)}) copy-start(bf16[192,768]{1,0:T(8,128)(2,1)} %param.46) | copy-start | bytes 884740
  0.7 47.5 %copy-start.99 = (bf16[3,768,192]{1,2,0:T(8,128)(2,1)S(1)}, bf16[3,768,192]{1,2,0:T(8,128)(2,1)}, u32[]{:S(2)}) copy-start(bf16[3,768,192]{1,2,0:T(8,128)(2,1)} %param.44) | copy-start | bytes 2654212
  4.1 26.5 %copy-start.109 = (f32[768]{0:T(1024)}, f32[768]{0:T(1024)S(1)}, u32[]{:S(2)}) copy-start(f32[768]{0:T(1024)S(1)} %get-tuple-element.191) | copy-start | bytes 9220
  5.4 178.7 %copy-start.58 = (bf16[320,768]{1,0:T(8,128)(2,1)}, bf16[320,768]{1,0:T(8,128)(2,1)S(1)}, u32[]{:S(2)}) copy-start(bf16[320,768]{1,0:T(8,128)(2,1)S(1)} %fusion.109) | copy-start | bytes 1474564
  5.4 44.3 %copy-start.137 = (s32[2]{0:T(128)S(1)}, s32[2]{0:T(128)}, u32[]{:S(2)}) copy-start(s32[2]{0:T(128)} %param.30) | copy-start | bytes 28
  5.4 173.5 %collective-permute-start = (bf16[320,768]{1,0:T(8,128)(2,1)S(1)}, bf16[320,768]{1,0:T(8,128)(2,1)}, u32[]{:S(2)}, u32[]{:S(2)}) collective-permute-start(bf16[320,768]{1,0:T(8,128)(2,1)S(1)} %fusion.109), channel_id=1, source_target_pairs={{0,1},{1,0},{2,3},{3,2},{4,5},{5,4},{6,7},{7,6},{8,9},{9,8},{10,11... | collective-permute-start | bytes 1474568 | tf_op jit(solution)/shard_map/ppermute | solution.py:63
  8.5 36.5 %copy-start.118 = (pred[4]{0:T(512)(128)(4,1)}, pred[4]{0:T(512)(128)(4,1)S(1)}, u32[]{:S(2)}) copy-start(pred[4]{0:T(512)(128)(4,1)S(1)} %compare_and_fusion) | copy-start | bytes 16
  163.1 12.3 %copy-start.115 = (f32[2,768]{1,0:T(2,128)S(1)}, f32[2,768]{1,0:T(2,128)}, u32[]{:S(2)}) copy-start(f32[2,768]{1,0:T(2,128)} %param.47) | copy-start | bytes 18436
  163.2 12.3 %copy-start.116 = (f32[2,768]{1,0:T(2,128)S(1)}, f32[2,768]{1,0:T(2,128)}, u32[]{:S(2)}) copy-start(f32[2,768]{1,0:T(2,128)} %param.48) | copy-start | bytes 18436
  169.5 12.4 %copy-start.19 = (bf16[4,192,768]{2,1,0:T(8,128)(2,1)}, bf16[4,192,768]{2,1,0:T(8,128)(2,1)S(1)}, u32[]{:S(2)}) copy-start(bf16[4,192,768]{2,1,0:T(8,128)(2,1)S(1)} %get-tuple-element.185) | copy-start | bytes 3538948
  169.5 14.6 %copy-start.4 = (bf16[4,192,768]{2,1,0:T(8,128)(2,1)}, bf16[4,192,768]{2,1,0:T(8,128)(2,1)S(1)}, u32[]{:S(2)}) copy-start(bf16[4,192,768]{2,1,0:T(8,128)(2,1)S(1)} %get-tuple-element.183) | copy-start | bytes 3538948
  174.0 12.8 %copy-start.12 = (bf16[320,768]{0,1:T(8,128)(2,1)}, bf16[320,768]{0,1:T(8,128)(2,1)S(1)}, u32[]{:S(2)}) copy-start(bf16[320,768]{0,1:T(8,128)(2,1)S(1)} %copy.70) | copy-start | bytes 1474564
  199.5 10.8 %copy-start.92 = (f32[320,1,768]{2,0,1:T(8,128)}, f32[320,1,768]{2,0,1:T(8,128)S(1)}, u32[]{:S(2)}) copy-start(f32[320,1,768]{2,0,1:T(8,128)S(1)} %fusion.59) | copy-start | bytes 2949124
  200.1 10.2 %copy-start.94 = (f32[320,1,768]{2,0,1:T(8,128)}, f32[320,1,768]{2,0,1:T(8,128)S(1)}, u32[]{:S(2)}) copy-start(f32[320,1,768]{2,0,1:T(8,128)S(1)} %fusion.60) | copy-start | bytes 2949124
  200.7 9.6 %copy-start.96 = (f32[320,1,768]{2,0,1:T(8,128)}, f32[320,1,768]{2,0,1:T(8,128)S(1)}, u32[]{:S(2)}) copy-start(f32[320,1,768]{2,0,1:T(8,128)S(1)} %fusion.61) | copy-start | bytes 2949124
  200.7 9.6 %copy-start.83 = (bf16[768,768]{1,0:T(8,128)(2,1)S(1)}, bf16[768,768]{1,0:T(8,128)(2,1)}, u32[]{:S(2)}) copy-start(bf16[768,768]{1,0:T(8,128)(2,1)} %refs_2_.1) | copy-start | bytes 3538948
  200.7 9.6 %copy-start.127 = (f32[768]{0:T(1024)S(1)}, f32[768]{0:T(1024)}, u32[]{:S(2)}) copy-start(f32[768]{0:T(1024)} %get-tuple-element.89) | copy-start | bytes 9220
  200.7 9.6 %copy-start.132 = (bf16[3,768,768]{2,1,0:T(8,128)(2,1)S(1)}, bf16[3,768,768]{2,1,0:T(8,128)(2,1)}, u32[]{:S(2)}) copy-start(bf16[3,768,768]{2,1,0:T(8,128)(2,1)} %get-tuple-element.39) | copy-start | bytes 10616836
  210.3 12.4 %copy-start.31 = (bf16[4,192,768]{2,1,0:T(8,128)(2,1)S(1)}, bf16[4,192,768]{2,1,0:T(8,128)(2,1)}, u32[]{:S(2)}) copy-start(bf16[4,192,768]{2,1,0:T(8,128)(2,1)} %get-tuple-element.119) | copy-start | bytes 3538948
  210.3 12.4 %copy-start.131 = (f32[768]{0:T(1024)S(1)}, f32[768]{0:T(1024)}, u32[]{:S(2)}) copy-start(f32[768]{0:T(1024)} %add.428) | copy-start | bytes 9220
  213.0 21.9 %copy-start.130 = (f32[768]{0:T(1024)S(1)}, f32[768]{0:T(1024)}, u32[]{:S(2)}) copy-start(f32[768]{0:T(1024)} %add.425) | copy-start | bytes 9220
  214.3 20.6 %collective-permute-start.1 = (bf16[320,768]{1,0:T(8,128)(2,1)}, bf16[320,768]{1,0:T(8,128)(2,1)}, u32[]{:S(2)}, u32[]{:S(2)}) collective-permute-start(bf16[320,768]{1,0:T(8,128)(2,1)} %add_convert_fusion.6), channel_id=1, source_target_pairs={{0,1},{1,0},{2,3},{3,2},{4,5},{5,4},{6,7},{7,6},{8,9},{9,8},{10,11... | collective-permute-start | bytes 1474568 | tf_op jit(solution)/shard_map/ppermute | solution.py:63
  225.5 15.2 %copy-start.6 = (bf16[4,192,768]{2,1,0:T(8,128)(2,1)S(1)}, bf16[4,192,768]{2,1,0:T(8,128)(2,1)}, u32[]{:S(2)}) copy-start(bf16[4,192,768]{2,1,0:T(8,128)(2,1)} %get-tuple-element.120) | copy-start | bytes 3538948
  260.1 8.6 %copy-start.82 = (bf16[768,768]{1,0:T(8,128)(2,1)S(1)}, bf16[768,768]{1,0:T(8,128)(2,1)}, u32[]{:S(2)}) copy-start(bf16[768,768]{1,0:T(8,128)(2,1)} %refs_5_.1) | copy-start | bytes 3538948
  260.1 8.6 %copy-start.125 = (f32[768]{0:T(1024)S(1)}, f32[768]{0:T(1024)}, u32[]{:S(2)}) copy-start(f32[768]{0:T(1024)} %get-tuple-element.200) | copy-start | bytes 9220
  260.1 8.6 %copy-start.134 = (bf16[3,768,768]{2,1,0:T(8,128)(2,1)S(1)}, bf16[3,768,768]{2,1,0:T(8,128)(2,1)}, u32[]{:S(2)}) copy-start(bf16[3,768,768]{2,1,0:T(8,128)(2,1)} %get-tuple-element.42) | copy-start | bytes 10616836
  260.1 8.6 %copy-start.135 = (bf16[320,768]{1,0:T(8,128)(2,1)S(1)}, bf16[320,768]{1,0:T(8,128)(2,1)}, u32[]{:S(2)}) copy-start(bf16[320,768]{1,0:T(8,128)(2,1)} %param.31) | copy-start | bytes 1474564
  280.1 11.5 %slice-start.3 = ((s8[9830400]{0:T(1024)(128)(4,1)}), s8[1441792]{0:T(1024)(128)(4,1)S(1)}, s32[]{:S(2)}) async-start(s8[9830400]{0:T(1024)(128)(4,1)} %bitcast.351), calls=%async_computation.3 | async-start | bytes 2883584
  283.6 8.1 %slice-start.5 = ((s8[9830400]{0:T(1024)(128)(4,1)}), s8[4194304]{0:T(1024)(128)(4,1)S(1)}, s32[]{:S(2)}) async-start(s8[9830400]{0:T(1024)(128)(4,1)} %bitcast.351), calls=%async_computation.5 | async-start | bytes 8388608
  283.6 8.1 %copy-start.44 = (bf16[320,768]{0,1:T(8,128)(2,1)S(1)}, bf16[320,768]{0,1:T(8,128)(2,1)}, u32[]{:S(2)}) copy-start(bf16[320,768]{0,1:T(8,128)(2,1)} %copy.75) | copy-start | bytes 1474564
  294.6 28.9 %copy-start.69 = (bf16[12,64,640]{2,1,0:T(8,128)(2,1)}, bf16[12,64,640]{2,1,0:T(8,128)(2,1)S(1)}, u32[]{:S(2)}) copy-start(bf16[12,64,640]{2,1,0:T(8,128)(2,1)S(1)} %get-tuple-element.172) | copy-start | bytes 2949124
  299.0 22.8 %copy-start.17 = (bf16[12,64,640]{2,1,0:T(8,128)(2,1)}, bf16[12,64,640]{2,1,0:T(8,128)(2,1)S(1)}, u32[]{:S(2)}) copy-start(bf16[12,64,640]{2,1,0:T(8,128)(2,1)S(1)} %multiply_convert_fusion.5) | copy-start | bytes 2949124
  326.0 25.5 %collective-permute-start.2 = (bf16[320,768]{1,0:T(8,128)(2,1)}, bf16[320,768]{1,0:T(8,128)(2,1)}, u32[]{:S(2)}, u32[]{:S(2)}) collective-permute-start(bf16[320,768]{1,0:T(8,128)(2,1)} %fusion.70), channel_id=1, source_target_pairs={{0,1},{1,0},{2,3},{3,2},{4,5},{5,4},{6,7},{7,6},{8,9},{9,8},{10,11... | collective-permute-start | bytes 1474568 | tf_op jit(solution)/shard_map/ppermute | solution.py:63
  345.4 10.8 %copy-start.133 = (bf16[3,768,768]{2,1,0:T(8,128)(2,1)S(1)}, bf16[3,768,768]{2,1,0:T(8,128)(2,1)}, u32[]{:S(2)}) copy-start(bf16[3,768,768]{2,1,0:T(8,128)(2,1)} %get-tuple-element.39) | copy-start | bytes 10616836
  363.9 11.8 %slice-start = ((s8[9830400]{0:T(1024)(128)(4,1)}), s8[1441792]{0:T(1024)(128)(4,1)S(1)}, s32[]{:S(2)}) async-start(s8[9830400]{0:T(1024)(128)(4,1)} %bitcast.349), calls=%async_computation | async-start | bytes 2883584
  378.7 23.6 %copy-start.67 = (bf16[12,64,640]{2,1,0:T(8,128)(2,1)}, bf16[12,64,640]{2,1,0:T(8,128)(2,1)S(1)}, u32[]{:S(2)}) copy-start(bf16[12,64,640]{2,1,0:T(8,128)(2,1)S(1)} %get-tuple-element.176) | copy-start | bytes 2949124
  382.9 18.4 %copy-start.15 = (bf16[12,64,640]{2,1,0:T(8,128)(2,1)}, bf16[12,64,640]{2,1,0:T(8,128)(2,1)S(1)}, u32[]{:S(2)}) copy-start(bf16[12,64,640]{2,1,0:T(8,128)(2,1)S(1)} %multiply_convert_fusion.4) | copy-start | bytes 2949124
  404.7 213.3 %collective-permute-start.3 = (bf16[320,768]{1,0:T(8,128)(2,1)}, bf16[320,768]{1,0:T(8,128)(2,1)}, u32[]{:S(2)}, u32[]{:S(2)}) collective-permute-start(bf16[320,768]{1,0:T(8,128)(2,1)} %fusion.71), channel_id=1, source_target_pairs={{0,1},{1,0},{2,3},{3,2},{4,5},{5,4},{6,7},{7,6},{8,9},{9,8},{10,11... | collective-permute-start | bytes 1474568 | tf_op jit(solution)/shard_map/ppermute | solution.py:63
  409.5 10.9 %collective-permute-start.9 = (f32[14,768]{1,0:T(8,128)S(1)}, f32[14,768]{1,0:T(8,128)S(1)}, u32[]{:S(2)}, u32[]{:S(2)}) collective-permute-start(f32[14,768]{1,0:T(8,128)S(1)} %concatenate.65), channel_id=1, source_target_pairs={{0,1},{1,0},{2,3},{3,2},{4,5},{5,4},{6,7},{7,6},{8,9},{9,8},{10,11... | collective-permute-start | bytes 129032 | tf_op jit(solution)/shard_map/ppermute | solution.py:63
  420.4 5.5 collective-permute-start.10
  425.9 2.5 collective-permute-start.11
  428.4 4.2 collective-permute-start.12
  432.6 185.4 %collective-permute-start.13 = (f32[14,768]{1,0:T(8,128)S(1)}, f32[14,768]{1,0:T(8,128)S(1)}, u32[]{:S(2)}, u32[]{:S(2)}) collective-permute-start(f32[14,768]{1,0:T(8,128)S(1)} %add.484), channel_id=1, source_target_pairs={{0,16},{4,20},{8,24},{12,28},{16,0},{20,4},{24,8},{28,12},{1,17},{... | collective-permute-start | bytes 129032 | tf_op jit(solution)/shard_map/ppermute | solution.py:63
  621.3 6.0 collective-permute-start.4
  627.3 5.0 collective-permute-start.5
  632.4 1.3 collective-permute-start.6
  633.7 4.2 collective-permute-start.7
  637.9 4.2 collective-permute-start.8
  (110 other events, 431.6 us)

commit v2 on v1

--- a/solution.py
+++ b/solution.py
@@ -117,25 +117,151 @@
     return pl.ds(pl.multiple_of(index * size, size), size)
 
 
-def gather_kernel(dp_size, *refs):
-    local = refs[:COUNT]
-    full = refs[COUNT : 2 * COUNT]
-    send, recv = refs[2 * COUNT :]
+def dot(left_side, right_side, contract=(1, 0)):
+    return lax.dot_general(
+        left_side,
+        right_side,
+        (((contract[0],), (contract[1],)), ((), ())),
+        preferred_element_type=F32,
+    )
+
+
+def blocks(count, size, body):
+    @pl.loop(0, count)
+    def _(i):
+        body(pl.ds(pl.multiple_of(i * size, size), size))
+
+
+def norm_parts(values):
+    center = values - jnp.mean(values, axis=-1, keepdims=True)
+    spread = jnp.mean(center * center, axis=-1, keepdims=True)
+    inverse = lax.rsqrt(spread + epsilon)
+    return center * inverse, inverse
+
+
+def norm_rows(source, gain, shift, target):
+    def body(rows):
+        unit, _ = norm_parts(source[rows, :])
+        target[rows, :] = (unit * gain + shift).astype(BF)
+
+    blocks(source.shape[0] // 32, 32, body)
+
+
+def project_rows(source, weight, bias, target):
+    def body(columns):
+        value = dot(source[...], weight[columns, :], (1, 1))
+        if bias is not None:
+            value = value + bias[:, columns]
+        target[:, columns] = value.astype(BF)
+
+    blocks(weight.shape[0] // 256, 256, body)
+
+
+def low_lanes(shape):
+    return lax.broadcasted_iota(jnp.int32, shape, 1) < HEAD_DIM
+
+
+def attend_pairs(first, last, query, key, value, key_bias, mixed, log_total):
+    rows = query.shape[0]
+
+    @pl.loop(first, last)
+    def _(p):
+        lanes = pl.ds(pl.multiple_of(p * 128, 128), 128)
+        query_pair = query[:, lanes]
+        key_pair = key[:, lanes]
+        value_pair = value[:, lanes]
+        low = low_lanes((rows, 128))
+        parts = []
+        for side in range(2):
+            chosen = low if side == 0 else ~low
+            one = jnp.where(chosen, query_pair, jnp.zeros_like(query_pair))
+            scores = dot(one, key_pair, (1, 1)) * HEAD_DIM ** (-0.5) + key_bias[...]
+            peak = jnp.max(scores, axis=1, keepdims=True)
+            exponent = jnp.exp(scores - peak)
+            total = jnp.sum(exponent, axis=1, keepdims=True)
+            probs = (exponent * (1.0 / total)).astype(BF)
+            parts.append(dot(probs, value_pair))
+            logs = jnp.broadcast_to(peak + jnp.log(total), (rows, 128))
+            log_total[p, side, :, :] = logs.T[0:8, :]
+        mixed[:, lanes] = jnp.where(low, parts[0], parts[1]).astype(BF)
+
+
+def attend_out(mixed, weight, bias, scale, resid, attn, middle):
+    def body(columns):
+        value = dot(mixed[...], weight[:, columns]) + bias[:, columns]
+        attn[:, columns] = value
+        middle[:, columns] = resid[:, columns] + scale[:, columns] * value
+
+    blocks(3, 256, body)
+
+
+def gelu_exact(values):
+    return 0.5 * values * (1.0 + lax.erf(values * (0.5**0.5)))
+
+
+def mlp_chunk(r, normed, up, up_bias, down, pre, hidden, mlp):
+    def body(columns):
+        value = dot(normed[...], up[r, :, columns]) + up_bias[r : r + 1, columns]
+        pre[r, :, columns] = value
+        unit = gelu_exact(value).astype(BF)
+        hidden[r, :, columns] = unit
+        mlp[...] += dot(unit, down[r, columns, :])
+
+    blocks(3, 256, body)
+
+KEPT = (
+    ("resid", (320, 768), F32),
+    ("normed", (640, 768), BF),
+    ("query", (320, 768), BF),
+    ("key", (640, 768), BF),
+    ("value", (640, 768), BF),
+    ("log_total", (6, 2, 8, 320), F32),
+    ("mixed", (320, 768), BF),
+    ("attn", (320, 768), F32),
+    ("middle", (320, 768), F32),
+    ("normed2", (320, 768), BF),
+    ("pre", (4, 320, 768), F32),
+    ("hidden", (4, 320, 768), BF),
+    ("mlp", (320, 768), F32),
+)
+KEPT_NAMES = [name for name, _, _ in KEPT]
+
+
+def forward_kernel(*refs):
+    refs = list(refs)
+
+    def take(count):
+        got = refs[:count]
+        del refs[:count]
+        return got
+
+    local = take(COUNT)
+    inputs, key_bias, small = take(3)
+    params = [take(4), take(4)]
+    full = take(COUNT)
+    kept_out = [dict(zip(KEPT_NAMES, take(len(KEPT)))) for _ in range(2)]
+    (output,) = take(1)
+    kept = [{name: ref.at[b] for name, ref in zip(KEPT_NAMES, refs)} for b in range(2)]
+    take(len(KEPT))
+    attn_w, up_w, down_w, small_in, in_bias, up_bias = take(6)
+    send, recv, other, load, store = take(5)
     size = local[0].shape[0] // PARTS
+    rows = inputs.shape[0]
     me = lax.rem(lax.axis_index("dp"), PARTS)
-    enter(dp_size)
-
-    def rows(mask):
+    flying = []
+    waiting = []
+
+    def part(mask):
         return piece_rows(flip(me, mask), size)
 
     def slab(i, mask):
-        return full[i].at[:, rows(mask)]
+        return full[i].at[:, part(mask)]
 
     def along_z(i):
         return [
             remote(
-                local[i].at[rows(0)],
-                full[i].at[r - 1, rows(0)],
+                local[i].at[part(0)],
+                full[i].at[r - 1, part(0)],
                 send.at[i, r - 1],
                 recv.at[i, r - 1],
                 {"mp": r},
@@ -147,8 +273,6 @@
         return remote(
             slab(i, mask), slab(i, mask), send.at[i, slot], recv.at[i, slot], {"dp": bit}
         )
-
-    flying = []
 
     def launch(copies):
         for copy in copies:
@@ -177,34 +301,184 @@
             landed(state[i])
             launch([along_dp(i, 8, second, 1), along_dp(i, 9, first | second, 1)])
 
-    for i in range(AHEAD):
-        state[i] = launch(along_z(i))
-    for t in range(COUNT + 2):
+    def step(t):
         for s in (0, 1, 2):
             if 0 <= t - s < COUNT:
                 stage(t - s, s)
-    for i in range(COUNT):
+
+    def complete(i):
         for slot, mask in ((6, 0), (7, ORDERS[i][0]), (8, ORDERS[i][1]), (9, 6)):
             along_dp(i, slot, mask, 1).wait_recv()
+
+    def chunk(i, r):
+        return local[i] if r == 0 else full[i].at[r - 1]
+
+    def load_attn(i):
+        copies = []
+        for kind in range(4):
+            for r in range(4):
+                copies.append(
+                    pltpu.make_async_copy(
+                        chunk(i, r).at[pl.ds(kind * 192, 192)],
+                        attn_w.at[kind, pl.ds(r * 192, 192)],
+                        load.at[0, kind * 4 + r],
+                    )
+                )
+        for copy in copies:
+            copy.start()
+        return copies
+
+    def load_mlp(i, target, slot):
+        copies = [
+            pltpu.make_async_copy(chunk(i, r), target.at[r], load.at[slot, r]) for r in range(4)
+        ]
+        for copy in copies:
+            copy.start()
+        return copies
+
+    def finish(copies):
+        for copy in copies:
+            copy.wait()
+
+    def save(b, *names):
+        for name in names:
+            copy = pltpu.make_async_copy(
+                kept[b][name], kept_out[b][name], store.at[b, KEPT_NAMES.index(name)]
+            )
+            copy.start()
+            waiting.append(copy)
+
+    def exchange(b):
+        copy = remote(
+            kept[b]["normed"].at[pl.ds(0, rows)],
+            kept[b]["normed"].at[pl.ds(rows, rows)],
+            other.at[0, 3 + b],
+            other.at[1, 3 + b],
+            {"mp": 1},
+        )
+        return launch([copy])
+
+    enter(lax.axis_size("dp"))
+    bias_in = launch(
+        [
+            remote(small.at[r], small_in.at[r - 1], other.at[0, r - 1], other.at[1, r - 1], {"mp": r})
+            for r in (1, 2, 3)
+        ]
+    )
+    for i in range(AHEAD):
+        state[i] = launch(along_z(i))
+
+    def widen(part_rows):
+        kept[0]["resid"][part_rows, :] = inputs[part_rows, :].astype(F32)
+
+    blocks(10, 32, widen)
+
+    for b in range(2):
+        k = kept[b]
+        gains, shifts, out_bias, scales = params[b]
+        base = 3 * b
+        norm_rows(k["resid"], gains[0:1, :], shifts[0:1, :], k["normed"].at[pl.ds(0, rows)])
+        save(b, "resid")
+        swapped = exchange(b)
+        if b == 0:
+            step(0)
+            step(1)
+            step(2)
+            landed(bias_in)
+            for c in range(2):
+                in_bias[c] = small[0, c, 0:8] + small_in[0, c] + small_in[1, c] + small_in[2, c]
+                up_bias[c, 0:1] = small[0, c, 0:1]
+                for r in (1, 2, 3):
+                    up_bias[c, r : r + 1] = small_in[r - 1, c, 0:1]
+        complete(base)
+        pending = load_attn(base)
+        project_bias = in_bias.at[b]
+        landed(swapped)
+        finish(pending)
+        project_rows(k["normed"].at[pl.ds(0, rows)], attn_w.at[0], project_bias.at[pl.ds(1, 1)], k["query"])
+        project_rows(k["normed"], attn_w.at[1], None, k["key"])
+        project_rows(k["normed"], attn_w.at[2], project_bias.at[pl.ds(2, 1)], k["value"])
+        save(b, "normed", "query", "key", "value")
+        pair_args = (k["query"], k["key"], k["value"], key_bias, k["mixed"], k["log_total"])
+        attend_pairs(0, 3, *pair_args)
+        step(3 * b + 3)
+        attend_pairs(3, 6, *pair_args)
+        save(b, "log_total", "mixed")
+        attend_out(
+            k["mixed"],
+            attn_w.at[3],
+            out_bias.at[pl.ds(0, 1)],
+            scales.at[pl.ds(0, 1)],
+            k["resid"],
+            k["attn"],
+            k["middle"],
+        )
+        norm_rows(k["middle"], gains[1:2, :], shifts[1:2, :], k["normed2"])
+        save(b, "attn", "middle", "normed2")
+        complete(base + 1)
+        pending = load_mlp(base + 1, up_w, 1)
+        step(3 * b + 4)
+        complete(base + 2)
+        pending = pending + load_mlp(base + 2, down_w, 2)
+        k["mlp"][...] = jnp.broadcast_to(out_bias[1:2, :], k["mlp"].shape)
+        finish(pending)
+        for r in range(4):
+            mlp_chunk(
+                r, k["normed2"], up_w, up_bias.at[b], down_w, k["pre"], k["hidden"], k["mlp"]
+            )
+            if r == 1:
+                step(3 * b + 5)
+        save(b, "pre", "hidden", "mlp")
+
+        def result(part_rows):
+            value = k["middle"][part_rows, :] + scales[1:2, :] * k["mlp"][part_rows, :]
+            if b == 0:
+                kept[1]["resid"][part_rows, :] = value
+            else:
+                output[part_rows, :] = value.astype(BF)
+
+        blocks(10, 32, result)
     for copy in flying:
         copy.wait_send()
-
-
-def gather_all(locals_):
-    dp_size = lax.axis_size("dp")
+    finish(waiting)
+
+
+def forward_all(locals_, inputs, key_bias, small, params):
     anywhere = pl.BlockSpec(memory_space=pl.ANY)
+    vmem = pl.BlockSpec(memory_space=pltpu.VMEM)
+    matrix = locals_[0].shape
+    kept_shapes = [jax.ShapeDtypeStruct(shape, kind) for _, shape, kind in KEPT]
     got = pl.pallas_call(
-        functools.partial(gather_kernel, dp_size),
-        out_shape=[jax.ShapeDtypeStruct((3,) + local.shape, BF) for local in locals_],
-        in_specs=[anywhere] * COUNT,
-        out_specs=[anywhere] * COUNT,
-        scratch_shapes=[
+        forward_kernel,
+        out_shape=[jax.ShapeDtypeStruct((3,) + matrix, BF)] * COUNT
+        + kept_shapes * 2
+        + [jax.ShapeDtypeStruct(inputs.shape, BF)],
+        in_specs=[anywhere] * COUNT + [vmem] * 11,
+        out_specs=[anywhere] * (COUNT + 2 * len(KEPT)) + [vmem],
+        scratch_shapes=[pltpu.VMEM((2,) + shape, kind) for _, shape, kind in KEPT]
+        + [
+            pltpu.VMEM((4,) + matrix, BF),
+            pltpu.VMEM((4,) + matrix, BF),
+            pltpu.VMEM((4,) + matrix, BF),
+            pltpu.VMEM((3, 2, 8, 768), F32),
+            pltpu.VMEM((2, 8, 768), F32),
+            pltpu.VMEM((2, 8, 768), F32),
             pltpu.SemaphoreType.DMA((COUNT, 10)),
             pltpu.SemaphoreType.DMA((COUNT, 10)),
+            pltpu.SemaphoreType.DMA((2, 5)),
+            pltpu.SemaphoreType.DMA((3, 16)),
+            pltpu.SemaphoreType.DMA((2, len(KEPT))),
         ],
-        compiler_params=pltpu.CompilerParams(collective_id=0, has_side_effects=True),
-    )(*locals_)
-    return [jnp.concatenate([local[None], rest]) for local, rest in zip(locals_, got)]
+        compiler_params=pltpu.CompilerParams(
+            collective_id=0, has_side_effects=True, vmem_limit_bytes=60 * 1024 * 1024
+        ),
+    )(*locals_, inputs, key_bias, small, *params)
+    full = got[:COUNT]
+    kept = [
+        dict(zip(KEPT_NAMES, got[COUNT + b * len(KEPT) : COUNT + (b + 1) * len(KEPT)]))
+        for b in range(2)
+    ]
+    return full, kept, got[-1]
 
 
 def reduce_kernel(dp_size, *refs):
@@ -436,60 +710,6 @@
     return values.reshape(values.shape[0], -1, HEAD_DIM)
 
 
-def forward_block(resid, key_valid, small, full):
-    gains, shifts, in_bias, out_bias, scales, up_bias = small
-    attn_w, up_w, down_w = full
-    normed, unit0, inverse0 = layer_norm(resid, gains[0], shifts[0])
-    normed = normed.astype(BF)
-    normed_all = jnp.concatenate([normed, swap(normed, "mp", 1)])
-    wq = attn_w[:, 0:192].reshape(768, 768)
-    wk = attn_w[:, 192:384].reshape(768, 768)
-    wv = attn_w[:, 384:576].reshape(768, 768)
-    wo = attn_w[:, 576:768].reshape(768, 768)
-    query = (matmul_nt(normed, wq) + in_bias[0]).astype(BF)
-    key = matmul_nt(normed_all, wk).astype(BF)
-    value = (matmul_nt(normed_all, wv) + in_bias[1]).astype(BF)
-    scores = jnp.einsum(
-        "qhd,khd->hqk", heads_of(query), heads_of(key), preferred_element_type=F32
-    ) * HEAD_DIM ** (-0.5)
-    scores = jnp.where(key_valid[None, None, :], scores, -1e30)
-    peak = jnp.max(scores, axis=-1, keepdims=True)
-    exponent = jnp.exp(scores - peak)
-    total = jnp.sum(exponent, axis=-1, keepdims=True)
-    probs = (exponent / total).astype(BF)
-    mixed = jnp.einsum("hqk,khd->qhd", probs, heads_of(value), preferred_element_type=F32)
-    mixed = mixed.reshape(query.shape).astype(BF)
-    log_total = peak + jnp.log(total)
-    attn = matmul(mixed, wo) + out_bias[0]
-    middle = resid + scales[0] * attn
-    normed2, unit1, inverse1 = layer_norm(middle, gains[1], shifts[1])
-    normed2 = normed2.astype(BF)
-    pre = jnp.stack([matmul(normed2, up_w[r]) + up_bias[r] for r in range(4)], axis=1)
-    hidden = gelu_exact(pre).astype(BF)
-    mlp = (
-        matmul(hidden.reshape(hidden.shape[0], -1), down_w.reshape(-1, 768)) + out_bias[1]
-    )
-    result = middle + scales[1] * mlp
-    kept = (
-        unit0,
-        inverse0,
-        normed_all,
-        query,
-        key,
-        value,
-        log_total,
-        mixed,
-        attn,
-        unit1,
-        inverse1,
-        normed2,
-        pre,
-        hidden,
-        mlp,
-    )
-    return result, kept
-
-
 def backward_block(grad, key_valid, small, full, kept):
     gains, shifts, in_bias, out_bias, scales, up_bias = small
     attn_w, up_w, down_w = full
@@ -625,13 +845,43 @@
     return [attn_local, up, down]
 
 
-def gather_small(project_bias, up_bias):
-    bias = lax.all_gather(
-        jnp.concatenate([project_bias.reshape(-1), up_bias]), "mp", axis=0, tiled=False
-    )
-    bias = relative(bias)
-    in_bias = bias[:, :384].reshape(4, 2, 192).swapaxes(0, 1).reshape(2, 768)
-    return in_bias, bias[:, 384:]
+def small_rows(weights):
+    p_bias, up_bias = weights[3], weights[8]
+    width = p_bias.shape[1]
+    rows = [
+        jnp.concatenate(
+            [
+                up_bias[None],
+                jnp.pad(p_bias, ((0, 0), (r * width, (3 - r) * width))),
+                jnp.zeros((5, 4 * width), F32),
+            ]
+        )
+        for r in range(4)
+    ]
+    return jnp.stack(rows)
+
+
+def unpack_kept(k, gains):
+    unit0, inverse0 = norm_parts(k["resid"])
+    unit1, inverse1 = norm_parts(k["middle"])
+    log_total = k["log_total"][:, :, 0].reshape(12, -1, 1)
+    return (
+        unit0,
+        inverse0,
+        k["normed"],
+        k["query"],
+        k["key"],
+        k["value"],
+        log_total,
+        k["mixed"],
+        k["attn"],
+        unit1,
+        inverse1,
+        k["normed2"],
+        k["pre"].swapaxes(0, 1),
+        k["hidden"].swapaxes(0, 1),
+        k["mlp"],
+    )
 
 
 def body(inputs, lengths, cotangent, *params):
@@ -644,28 +894,32 @@
         [half * rows + jnp.arange(rows), (1 - half) * rows + jnp.arange(rows)]
     )
     key_valid = position < length
-
-    def prepare(weights):
-        gains, shifts, p_in, p_bias, p_out, out_bias, scales, up, up_bias, down = weights
-        in_bias, up_bias_all = gather_small(p_bias, up_bias)
-        return (gains, shifts, in_bias, out_bias, scales, up_bias_all)
-
-    full = gather_all(local_block(student) + local_block(teacher))
+    key_bias = jnp.where(key_valid, 0.0, -1e30).astype(F32)[None]
+    locals_ = local_block(student) + local_block(teacher)
+    small = jnp.stack([small_rows(student), small_rows(teacher)], axis=1)
+    replicated = [
+        weights[position_] for weights in (student, teacher) for position_ in (0, 1, 5, 6)
+    ]
+    got, kept, output = forward_all(locals_, inputs, key_bias, small, replicated)
+    full = [jnp.concatenate([local[None], rest]) for local, rest in zip(locals_, got)]
     student_full, teacher_full = full[:3], full[3:]
-    student_small = prepare(student)
-    teacher_small = prepare(teacher)
-    start_rows = inputs.astype(F32)
-    student_out, student_kept = forward_block(start_rows, key_valid, student_small, student_full)
-    teacher_out, teacher_kept = forward_block(student_out, key_valid, teacher_small, teacher_full)
+
+    def trimmed(weights):
+        return (weights[0], weights[1], None, weights[5], weights[6], None)
+
     grad_mid, teacher_large, teacher_rest = backward_block(
-        cotangent.astype(F32), key_valid, teacher_small, teacher_full, teacher_kept
+        cotangent.astype(F32),
+        key_valid,
+        trimmed(teacher),
+        teacher_full,
+        unpack_kept(kept[1], teacher[0]),
     )
     grad_input, student_large, student_rest = backward_block(
-        grad_mid, key_valid, student_small, student_full, student_kept
+        grad_mid, key_valid, trimmed(student), student_full, unpack_kept(kept[0], student[0])
     )
     reduced = reduce_all(teacher_large + student_large)
     return (
-        (teacher_out.astype(BF), grad_input.astype(BF))
+        (output, grad_input.astype(BF))
         + arrange(reduced[3:], student_rest)
         + arrange(reduced[:3], teacher_rest)
     )

time: 656 us -> 582 us (0.89)
  Pallas kernels: 288 us -> 329 us
  matrix products: 147 us -> 111 us
  other arithmetic: 75.2 us -> 39.3 us
  blocking collectives: 32.2 us -> 0 us
  waiting for transfers between devices: 22.1 us -> 9.9 us
    pallas_call x1, Pallas kernels: 113 us -> 153 us  [forward_all(): pl.pallas_call(forward_kernel, out_shape=[jax.ShapeDtypeStruct((3,) + mat...]
    all_gather x2 -> x0, blocking collectives: 32.2 us -> none  [gather_small(): lax.all_gather(jnp.concatenate([project_bias.reshape(-1), up_bias]), 'mp'...]
    convert_element_type x6 -> x0, other arithmetic: 20.8 us -> none  [the longest x2 18 us: forward_block(): hidden = gelu_exact(pre).astype(BF)]
    dot_general x22 -> x10, matrix products: 29.4 us -> 16.6 us  [matmul(): return jnp.dot(left_side, right_side, preferred_element_type=F32)]
    ppermute x14 -> x12, waiting for transfers between devices: 22.1 us -> 9.9 us  [swap(): return lax.ppermute(source, axis, [(i, i ^ bit) for i in range(count)])]
    pallas_call x0 -> x6, local copies, waits for them, and re-layouts: none -> 11.9 us  [forward_all(): pl.pallas_call(forward_kernel, out_shape=[jax.ShapeDtypeStruct((3,) + mat...]
    dot_general x18 -> x12, matrix products: 29.3 us -> 18.1 us  [matmul_nt(): lax.dot_general(left_side, right_side, (((1,), (1,)), ((), ())), preferre...]
    convert_element_type x6 -> x0, local copies, waits for them, and re-layouts: 9.07 us -> none  [the longest x2 4.49 us: forward_block(): value = (matmul_nt(normed_all, wv) + in_bias[1]).astype(BF)]
  transfers between devices with their start and end apart: 14 -> 12, of which waited for: 7 -> 7; matrix products, arithmetic and copies ran while one was open for 13% -> 15% of each run, Pallas kernels for 44% -> 31%
where the time goes in v2:
time: 582 us; the launch traced here: 572 us
  Pallas kernels  329 us (57%)
  matrix products  111 us (19%)
  local copies, waits for them, and re-layouts  58.6 us (10%)
  other arithmetic  39.3 us (7%)
  starting transfers between devices  21.7 us (4%)
  waiting for transfers between devices  9.9 us (2%)
    pallas_call x1, Pallas kernels, reduce_all(): pl.pallas_call(functools.partial(reduce_kernel, dp_size), out_shape=[jax....  176 us
    pallas_call x1, Pallas kernels, forward_all(): pl.pallas_call(forward_kernel, out_shape=[jax.ShapeDtypeStruct((3,) + mat...  153 us
    dot_general x24, matrix products, matmul_tn(): lax.dot_general(left_side, right_side, (((0,), (0,)), ((), ())), preferre...  41.7 us
    unnamed x189, local copies, waits for them, and re-layouts  22 us
    ppermute x12, starting transfers between devices, swap(): return lax.ppermute(source, axis, [(i, i ^ bit) for i in range(count)])  21.7 us
    dot_general x12, matrix products, matmul_nt(): lax.dot_general(left_side, right_side, (((1,), (1,)), ((), ())), preferre...  18.1 us
    dot_general x10, matrix products, matmul(): return jnp.dot(left_side, right_side, preferred_element_type=F32)  16.6 us
    pallas_call x6, local copies, waits for them, and re-layouts, forward_all(): pl.pallas_call(forward_kernel, out_shape=[jax.ShapeDtypeStruct((3,) + mat...  11.9 us
  transfers between devices with their start and end apart: 12, of which 7 were waited for; matrix products, arithmetic and copies ran while one was open for 15% of the time, Pallas kernels for 31%

profile of v2, /device:TPU:0, one launch (start us, length us, event | category | flops | bytes accessed | tf_op | source)
XLA Modules:
  0.0 572.0 jit_solution(1363888863464786085)
XLA Ops:
  7.9 3.6 fusion.112
  11.5 152.6 %shard_map.390 = (bf16[3,768,768]{2,1,0:T(8,128)(2,1)}, bf16[3,768,768]{2,1,0:T(8,128)(2,1)}, bf16[3,768,768]{2,1,0:T(8,128)(2,1)}, bf16[3,768,768]{2,1,0:T(8,12...) custom-call(bf16[768,768]{1,0:T(8,128)(2,1)} %get-tuple-element.210., ...), custom_call_target="tpu_custom_call" | custom-call | tf_op jit(solution)/shard_map/pallas_call | solution.py:451
  164.1 5.5 convert_reduce_fusion
  172.6 2.4 multiply_reduce_fusion.3
  183.0 2.2 copy.64
  187.8 2.9 convert_reduce_fusion.2
  190.7 3.7 multiply_reduce_fusion.1
  194.4 2.9 multiply_convert_fusion.1
  202.8 2.3 convert_reduce_fusion.4
  210.8 1.9 fusion.43
  212.7 1.9 fusion.36
  220.9 2.3 copy.65
  223.2 2.1 copy.66
  225.3 2.4 copy.68
  230.1 2.9 fusion.121
  234.9 2.1 convolution_convert_fusion.22
  237.0 2.1 convolution_convert_fusion.23
  239.1 1.9 convolution_convert_fusion.10
  241.4 2.1 convolution_add_fusion.8
  247.2 2.6 pad_maximum_fusion.2.refs_2_
  251.2 2.7 pad_maximum_fusion.1.refs_1_
  255.3 2.5 pad_maximum_fusion.refs_0_
  257.8 5.3 fusion.123
  263.1 2.2 multiply_reduce_fusion.4
  268.1 3.8 convert_reduce_fusion.1
  279.0 7.3 %convert_reduce_fusion.3 = (f32[12,64]{1,0:T(8,128)S(1)}, bf16[12,64,640]{2,1,0:T(8,128)(2,1)}) fusion(bf16[320,12,64]{0,2,1:T(8,128)(2,1)S(1)} %bitcast.367, f32[12,320,640]{2,1,0:T(8,128)} %fusion.123, f32[12,320]{1,0:T(8,128)S(1)} %sub.143, pred[640]{0:T(1024)(128)(4,1)S(1)} %add_compare_fusion), kind=kOutput, calls=%fused_computation.61 | convolution fusion | flops 325876992 | bytes 11324032 | tf_op jit(solution)/shard_map/hqk,qhd->khd/dot_general | solution.py:763
  286.3 7.3 %multiply_reduce_fusion = (f32[12,320]{1,0:T(8,128)S(1)}, f32[12,320,640]{2,1,0:T(8,128)S(1)}) fusion(f32[12,320,640]{2,1,0:T(8,128)} %fusion.123, f32[12,320]{1,0:T(8,128)S(1)} %sub.143, pred[640]{0:T(1024)(128)(4,1)S(1)} %add_compare_fusion, bf16[320,12,64]{0,2,1:T(8,128)(2,1)S(1)} %bitcast.368, bf16[640,12,64]{0,2,1:T(8,128)(2,1)S(1)} %bitcast.363), kind=kOutput, calls=%fused_computation.5 | convolution fusion | flops 326856960 | bytes 21166720 | tf_op jit(solution)/shard_map/qhd,khd->hqk/dot_general | solution.py:760
  293.6 2.9 multiply_convert_fusion
  296.5 2.3 convert_reduce_fusion.5
  313.0 2.1 collective-permute-start.7
  315.1 2.0 convolution_convert_fusion.1
  317.1 2.7 convolution_convert_fusion.20
  325.2 2.6 pad_maximum_fusion.5.refs_5_
  329.3 2.7 pad_maximum_fusion.4.refs_4_
  332.9 3.0 collective-permute-start.8
  339.1 2.5 pad_maximum_fusion.3.refs_3_
  341.5 3.7 collective-permute-start.10
  347.6 2.2 collective-permute-start.11
  351.4 176.4 %shard_map.391 = (f32[768,768]{1,0:T(8,128)}, f32[768,768]{1,0:T(8,128)}, f32[768,768]{1,0:T(8,128)}, f32[768,768]{1,0:T(8,128)}, f32[768,768]{1,0:T(8,128)}, /*index=5*/f32[768,768]{1,0:T(8,128)}) custom-call(bf16[4,768,768]{2,1,0:T(8,128)(2,1)} %pad_maximum_fusion.refs_0_, bf16[4,768,768]{2,1,0:T(8,128)(2,1)} %pad_maximum_fusion.1.refs_1_, ...), custom_call_target="tpu_custom_call" | custom-call | tf_op jit(solution)/shard_map/pallas_call | solution.py:671
  527.9 2.9 slice.290
  530.8 1.9 slice.292
  535.1 3.3 multiply_reduce_fusion.8
  538.5 3.0 collective-permute-start.2
  543.9 2.9 collective-permute-start.3
  550.2 2.8 collective-permute-start.5
  553.0 2.1 collective-permute-done.5
  555.9 2.5 add_convert_fusion
  561.9 3.4 copy.77
  (357 shorter events, 106.5 us)
Async XLA Ops:
  11.5 152.6 %copy-start.54 = (bf16[768,768]{1,0:T(8,128)(2,1)S(1)}, bf16[768,768]{1,0:T(8,128)(2,1)}, u32[]{:S(2)}) copy-start(bf16[768,768]{1,0:T(8,128)(2,1)} %refs_5_.1) | copy-start | bytes 3538948
  11.5 152.6 %copy-start.65 = (bf16[320,768]{1,0:T(8,128)(2,1)S(1)}, bf16[320,768]{1,0:T(8,128)(2,1)}, u32[]{:S(2)}) copy-start(bf16[320,768]{1,0:T(8,128)(2,1)} %param.29) | copy-start | bytes 1474564
  164.1 5.6 copy-start.19
  164.1 6.1 %copy-start.32 = (bf16[3,768,768]{2,1,0:T(8,128)(2,1)S(1)}, bf16[3,768,768]{2,1,0:T(8,128)(2,1)}, u32[]{:S(2)}) copy-start(bf16[3,768,768]{2,1,0:T(8,128)(2,1)} %get-tuple-element.67) | copy-start | bytes 10616836
  190.7 8.9 %copy-start.33 = (bf16[12,64,640]{2,1,0:T(8,128)(2,1)}, bf16[12,64,640]{2,1,0:T(8,128)(2,1)S(1)}, u32[]{:S(2)}) copy-start(bf16[12,64,640]{2,1,0:T(8,128)(2,1)S(1)} %get-tuple-element.197) | copy-start | bytes 2949124
  202.7 60.3 %collective-permute-start = (bf16[320,768]{1,0:T(8,128)(2,1)}, bf16[320,768]{1,0:T(8,128)(2,1)}, u32[]{:S(2)}, u32[]{:S(2)}) collective-permute-start(bf16[320,768]{1,0:T(8,128)(2,1)} %fusion.54), channel_id=1, source_target_pairs={{0,1},{1,0},{2,3},{3,2},{4,5},{5,4},{6,7},{7,6},{8,9},{9,8},{10,11... | collective-permute-start | bytes 1474568 | tf_op jit(solution)/shard_map/ppermute | solution.py:63
  208.9 3.8 copy-start.67
  208.9 3.8 copy-start.82
  216.4 3.6 copy-start.3
  220.9 9.2 %copy-start.26 = (bf16[12,64,320]{2,1,0:T(8,128)(2,1)S(1)}, bf16[12,64,320]{2,1,0:T(8,128)(2,1)}, u32[]{:S(2)}) copy-start(bf16[12,64,320]{2,1,0:T(8,128)(2,1)} %get-tuple-element.199) | copy-start | bytes 1474564
  230.1 4.7 copy-start.34
  247.2 3.7 copy-start.38
  247.2 4.0 copy-start.39
  251.2 3.7 copy-start.44
  251.2 4.0 copy-start.45
  257.8 5.3 copy-start.4
  257.8 5.3 copy-start.17
  257.8 5.3 copy-start.64
  263.1 4.1 copy-start.79
  267.2 4.8 copy-start.69
  268.1 3.9 copy-start.20
  268.1 4.5 copy-start.31
  279.0 7.3 %copy-start.21 = (bf16[640,768]{0,1:T(8,128)(2,1)S(1)}, bf16[640,768]{0,1:T(8,128)(2,1)}, u32[]{:S(2)}) copy-start(bf16[640,768]{0,1:T(8,128)(2,1)} %copy.68) | copy-start | bytes 2949124
  286.2 7.3 %slice-start = ((s8[9830400]{0:T(1024)(128)(4,1)}), s8[4194304]{0:T(1024)(128)(4,1)S(1)}, s32[]{:S(2)}) async-start(s8[9830400]{0:T(1024)(128)(4,1)} %bitcast.339), calls=%async_computation | async-start | bytes 8388608
  286.2 7.3 %slice-start.1 = ((s8[9830400]{0:T(1024)(128)(4,1)}), s8[4194304]{0:T(1024)(128)(4,1)S(1)}, s32[]{:S(2)}) async-start(s8[9830400]{0:T(1024)(128)(4,1)} %bitcast.339), calls=%async_computation.1 | async-start | bytes 8388608
  286.3 7.3 %slice-start.2 = ((s8[9830400]{0:T(1024)(128)(4,1)}), s8[1441792]{0:T(1024)(128)(4,1)S(1)}, s32[]{:S(2)}) async-start(s8[9830400]{0:T(1024)(128)(4,1)} %bitcast.339), calls=%async_computation.2 | async-start | bytes 2883584
  304.1 3.6 copy-start.70
  304.1 3.6 copy-start.80
  313.0 19.8 %collective-permute-start.7 = (f32[14,768]{1,0:T(8,128)S(1)}, f32[14,768]{1,0:T(8,128)S(1)}, u32[]{:S(2)}, u32[]{:S(2)}) collective-permute-start(f32[14,768]{1,0:T(8,128)S(1)} %concatenate.97), channel_id=1, source_target_pairs={{0,1},{1,0},{2,3},{3,2},{4,5},{5,4},{6,7},{7,6},{8,9},{9,8},{10,11... | collective-permute-start | bytes 129032 | tf_op jit(solution)/shard_map/ppermute | solution.py:63
  325.2 209.9 %collective-permute-start.1 = (bf16[320,768]{1,0:T(8,128)(2,1)}, bf16[320,768]{1,0:T(8,128)(2,1)}, u32[]{:S(2)}, u32[]{:S(2)}) collective-permute-start(bf16[320,768]{1,0:T(8,128)(2,1)} %fusion.55), channel_id=1, source_target_pairs={{0,1},{1,0},{2,3},{3,2},{4,5},{5,4},{6,7},{7,6},{8,9},{9,8},{10,11... | collective-permute-start | bytes 1474568 | tf_op jit(solution)/shard_map/ppermute | solution.py:63
  325.2 3.7 copy-start.48
  325.2 4.0 copy-start.49
  332.0 7.0 %copy-start.40 = (bf16[1,768,768]{2,1,0:T(8,128)(2,1)S(1)}, bf16[1,768,768]{2,1,0:T(8,128)(2,1)}, u32[]{:S(2)}) copy-start(bf16[1,768,768]{2,1,0:T(8,128)(2,1)} %fusion.44) | copy-start | bytes 3538948
  332.0 7.0 %copy-start.41 = (bf16[1,768,768]{2,1,0:T(8,128)(2,1)S(1)}, bf16[1,768,768]{2,1,0:T(8,128)(2,1)}, u32[]{:S(2)}) copy-start(bf16[1,768,768]{2,1,0:T(8,128)(2,1)} %fusion.45) | copy-start | bytes 3538948
  332.9 5.2 collective-permute-start.8
  338.1 7.2 %copy-start.18 = (bf16[4,192,768]{2,1,0:T(8,128)(2,1)S(1)}, bf16[4,192,768]{2,1,0:T(8,128)(2,1)}, u32[]{:S(2)}) copy-start(bf16[4,192,768]{2,1,0:T(8,128)(2,1)} %get-tuple-element.142) | copy-start | bytes 3538948
  338.1 7.2 %copy-start.25 = (bf16[12,64,320]{2,1,0:T(8,128)(2,1)S(1)}, bf16[12,64,320]{2,1,0:T(8,128)(2,1)}, u32[]{:S(2)}) copy-start(bf16[12,64,320]{2,1,0:T(8,128)(2,1)} %get-tuple-element.203) | copy-start | bytes 1474564
  338.1 3.4 collective-permute-start.9
  341.5 6.1 %collective-permute-start.10 = (f32[14,768]{1,0:T(8,128)S(1)}, f32[14,768]{1,0:T(8,128)S(1)}, u32[]{:S(2)}, u32[]{:S(2)}) collective-permute-start(f32[14,768]{1,0:T(8,128)S(1)} %add.230), channel_id=1, source_target_pairs={{0,8},{4,12},{8,0},{12,4},{16,24},{20,28},{24,16},{28,20},{1,9},{5... | collective-permute-start | bytes 129032 | tf_op jit(solution)/shard_map/ppermute | solution.py:63
  347.6 187.4 %collective-permute-start.11 = (f32[14,768]{1,0:T(8,128)S(1)}, f32[14,768]{1,0:T(8,128)S(1)}, u32[]{:S(2)}, u32[]{:S(2)}) collective-permute-start(f32[14,768]{1,0:T(8,128)S(1)} %add.231), channel_id=1, source_target_pairs={{0,16},{4,20},{8,24},{12,28},{16,0},{20,4},{24,8},{28,12},{1,17},{... | collective-permute-start | bytes 129032 | tf_op jit(solution)/shard_map/ppermute | solution.py:63
  527.8 4.9 copy-start.27
  538.5 5.4 collective-permute-start.2
  543.9 17.3 %copy-start.68 = (bf16[320,768]{1,0:T(8,128)(2,1)S(1)}, bf16[320,768]{1,0:T(8,128)(2,1)}, u32[]{:S(2)}) copy-start(bf16[320,768]{1,0:T(8,128)(2,1)} %get-tuple-element.238) | copy-start | bytes 1474564
  543.9 5.1 collective-permute-start.3
  549.0 1.3 collective-permute-start.4
  550.2 4.8 collective-permute-start.5
  555.1 4.2 collective-permute-start.6
  561.9 3.4 copy-start.30
  (56 other events, 124.0 us)
